TPU v7x, 256 devices: a whole 4x4x8 slice. The times are simulated.
256 devices in a mesh: ctx: 32 (over y_lo, z, core), ch: 8 (over x, y_hi).
Axes of the slice: x: 4, y: 4 (y_hi: 2, y_lo: 2; y = y_hi * 2 + y_lo), z: 8, core: 2. Of those that a mesh axis runs over, the one named last changes fastest.
Arguments:
- inputs: bfloat16 [8192, 4096], P('ctx', 'ch'), may hold values from -6 to 6
- in_weight: bfloat16 [4096, 3, 2048], P(None, None, 'ch'), may hold values from -0.09375 to 0.09375
- short_kernel: float32 [3, 3, 2048], P(None, None, 'ch'), may hold values from -3 to 3
- long_filter: float32 [8192, 2048], P('ctx', 'ch'), may hold values from -4 to 4
- skip_gain: float32 [2048], P('ch'), may hold values from -4 to 4
- out_weight: bfloat16 [2048, 4096], P(None, 'ch'), may hold values from -0.125 to 0.125
Outputs:
- mixed: bfloat16 [8192, 4096], P('ctx', 'ch')
All inputs are finite; a program needn't handle non-finite values.
Results may differ from a plain program's by a relative error of at most 0.005.
Values may be sent and summed in bfloat16 or wider, within the bound.
A program may use at most 64 MiB of HBM per device.

v0:
```python
import math

import jax
import jax.numpy as jnp
from jax import lax
from jax.sharding import PartitionSpec as P

HIGH = lax.Precision.HIGHEST


def from_partner(block, axis, stride):
    count = lax.axis_size(axis)
    route = []
    for low in range(count):
        high = low | 1 << stride
        if high != low and high < count:
            route += [(low, high), (high, low)]
    return lax.ppermute(block, axis, route)


def shifted(value, axis, steps):
    count = lax.axis_size(axis)
    initial, last = (max(0, -steps), min(count, count - steps))
    return lax.ppermute(value, axis, [(source, source + steps) for source in range(initial, last)])


def phase(numer, denom):
    angle = (numer % denom).astype(jnp.float32) * (2.0 * math.pi / denom)
    return (jnp.cos(angle), jnp.sin(angle))


def row_transform(cosine, sine, real_part, imag_part, forward):
    shape = real_part.shape
    left = real_part.reshape(shape[0], -1)
    right = imag_part.reshape(shape[0], -1)
    cos_real = jnp.dot(cosine, left, precision=HIGH, preferred_element_type=jnp.float32)
    sin_imag = jnp.dot(sine, right, precision=HIGH, preferred_element_type=jnp.float32)
    cos_imag = jnp.dot(cosine, right, precision=HIGH, preferred_element_type=jnp.float32)
    sin_real = jnp.dot(sine, left, precision=HIGH, preferred_element_type=jnp.float32)
    if forward:
        return ((cos_real + sin_imag).reshape(shape), (cos_imag - sin_real).reshape(shape))
    return ((cos_real - sin_imag).reshape(shape), (cos_imag + sin_real).reshape(shape))


def level_count():
    return lax.axis_size("ctx").bit_length() - 1


def forward_butterfly(signal, position, parts_count):
    cos_first, sin_first = phase(position, 2 * parts_count)
    real_part = jnp.stack([signal, signal * cos_first], 1)
    imag_part = jnp.stack([jnp.zeros_like(signal), -signal * sin_first], 1)
    levels = level_count()
    for level in reversed(range(levels)):
        half = 1 << level
        other_real, other_imag = from_partner((real_part, imag_part), "ctx", level)
        upper = position >> level & 1 == 1
        cosine, sine = phase(position % half, 2 * half)
        diff_real = other_real - real_part
        diff_imag = other_imag - imag_part
        turned_real = diff_real * cosine + diff_imag * sine
        turned_imag = diff_imag * cosine - diff_real * sine
        real_part = jnp.where(upper, turned_real, real_part + other_real)
        imag_part = jnp.where(upper, turned_imag, imag_part + other_imag)
    reversed_index = jnp.zeros((), jnp.int32)
    for level in range(levels):
        reversed_index = reversed_index + ((position >> level & 1) << levels - 1 - level)
    frequency = 2 * reversed_index + jnp.arange(2, dtype=jnp.int32)
    return (real_part, imag_part, frequency)


def inverse_butterfly(real_part, imag_part, position, parts_count):
    for level in range(level_count()):
        half = 1 << level
        other_real, other_imag = from_partner((real_part, imag_part), "ctx", level)
        upper = position >> level & 1 == 1
        cosine, sine = phase(position % half, 2 * half)
        lower_real = real_part + other_real * cosine - other_imag * sine
        lower_imag = imag_part + other_imag * cosine + other_real * sine
        upper_real = other_real - (real_part * cosine - imag_part * sine)
        upper_imag = other_imag - (imag_part * cosine + real_part * sine)
        real_part = jnp.where(upper, upper_real, lower_real)
        imag_part = jnp.where(upper, upper_imag, lower_imag)
    cos_last, sin_last = phase(position, 2 * parts_count)
    return real_part[:, 0] + cos_last * real_part[:, 1] - sin_last * imag_part[:, 1]


def long_convolution(gated, long_filter):
    row_count, chan_count = gated.shape
    parts_count = lax.axis_size("ctx")
    position = lax.axis_index("ctx")
    total = 2 * parts_count * row_count
    signal = jnp.concatenate([gated, long_filter], axis=1)
    real_part, imag_part, frequency = forward_butterfly(signal, position, parts_count)
    offsets = jnp.arange(row_count, dtype=jnp.int32)[:, None]
    twist_cos, twist_sin = phase(offsets * frequency[None, :], total)
    twist_cos = twist_cos[:, :, None]
    twist_sin = twist_sin[:, :, None]
    turned_real = real_part * twist_cos + imag_part * twist_sin
    turned_imag = imag_part * twist_cos - real_part * twist_sin
    grid_row = jnp.arange(row_count, dtype=jnp.int32)
    table_cos, table_sin = phase(grid_row[:, None] * grid_row[None, :], row_count)
    spec_real, spec_imag = row_transform(table_cos, table_sin, turned_real, turned_imag, True)
    value_real = spec_real[:, :, :chan_count]
    value_imag = spec_imag[:, :, :chan_count]
    filter_real = spec_real[:, :, chan_count:]
    filter_imag = spec_imag[:, :, chan_count:]
    prod_real = value_real * filter_real - value_imag * filter_imag
    prod_imag = value_real * filter_imag + value_imag * filter_real
    back_real, back_imag = row_transform(table_cos, table_sin, prod_real, prod_imag, False)
    untwist_real = back_real * twist_cos - back_imag * twist_sin
    untwist_imag = back_imag * twist_cos + back_real * twist_sin
    result = inverse_butterfly(untwist_real, untwist_imag, position, parts_count)
    return result * (1.0 / total)


def shards(inputs, in_weight, short_kernel, long_filter, skip_gain, out_weight):
    row_count = inputs.shape[0]
    width = in_weight.shape[0]
    chan_count = in_weight.shape[2]
    flat_weight = in_weight.reshape(width, 3 * chan_count)
    weight_rows = flat_weight
    projected = jnp.dot(
        lax.all_gather(inputs, "ch", axis=1, tiled=True),
        weight_rows,
        preferred_element_type=jnp.float32,
    )
    earlier = shifted(projected[row_count - 2 :], "ctx", 1)
    padded = jnp.concatenate([earlier, projected], axis=0)
    taps = short_kernel.reshape(3, 3 * chan_count)
    streams = taps[0] * padded[2:] + taps[1] * padded[1:-1] + taps[2] * padded[:-2]
    first_gate = streams[:, :chan_count]
    second_gate = streams[:, chan_count : 2 * chan_count]
    value = streams[:, 2 * chan_count :]
    gated = first_gate * value
    conv = long_convolution(gated, long_filter)
    gated_out = (second_gate * (conv + skip_gain * gated)).astype(jnp.bfloat16)
    weight_rows = out_weight
    mixed = jnp.dot(
        lax.all_gather(gated_out, "ch", axis=1, tiled=True),
        weight_rows,
        preferred_element_type=jnp.float32,
    )
    return mixed.astype(jnp.bfloat16)


def solution(mesh):
    placed = (
        P("ctx", "ch"),
        P(None, None, "ch"),
        P(None, None, "ch"),
        P("ctx", "ch"),
        P("ch"),
        P(None, "ch"),
    )
    return jax.shard_map(
        shards, mesh=mesh, in_specs=placed, out_specs=P("ctx", "ch"), check_vma=False
    )
```

profile of v0, /device:TPU:6, one launch (start us, length us, event | category | flops | bytes accessed | tf_op | source)
XLA Modules:
  0.0 658.1 jit_solution(12536584868737069899)
XLA Ops:
  7.3 8.6 %copy.7 = bf16[4096,3,256]{0,2,1:T(8,128)(2,1)} copy(bf16[4096,3,256]{2,0,1:T(8,128)(2,1)} %param.7) | data formatting | bytes 12582912 | tf_op args[1]
  15.9 59.2 %all-gather.3.cloned.1.call-done = bf16[256,4096]{1,0:T(8,128)(2,1)} async-done(((bf16[256,512]{1,0:T(8,128)(2,1)}), bf16[256,4096]{1,0:T(8,128)(2,1)}) %all-gather.3.cloned.1.call-update) | async-done | bytes 2097168 | tf_op jit(solution)/shard_map/all_gather | solution.py:124
  75.1 5.3 fusion.76
  85.6 5.5 collective-permute-start.1
  92.4 23.1 %collective-permute-done.1 = f32[256,2,512]{2,0,1:T(8,128)} collective-permute-done((f32[256,2,512]{2,0,1:T(8,128)}, f32[256,2,512]{2,0,1:T(8,128)}, u32[]{:S(2)}, u32[]{:S(2)}) %collective-permute-start.1) | collective-permute-done | bytes 1048608 | tf_op jit(solution)/shard_map/ppermute | solution.py:18
  115.6 20.2 %collective-permute-done.2 = f32[256,2,512]{2,0,1:T(8,128)} collective-permute-done((f32[256,2,512]{2,0,1:T(8,128)}, f32[256,2,512]{2,0,1:T(8,128)}, u32[]{:S(2)}, u32[]{:S(2)}) %collective-permute-start.2) | collective-permute-done | bytes 1048608 | tf_op jit(solution)/shard_map/ppermute | solution.py:18
  135.7 3.4 add_select_fusion.9
  139.2 4.8 collective-permute-start.3
  145.3 26.4 %collective-permute-done.3 = f32[256,2,512]{2,0,1:T(8,128)S(1)} collective-permute-done((f32[256,2,512]{2,0,1:T(8,128)}, f32[256,2,512]{2,0,1:T(8,128)S(1)}, u32[]{:S(2)}, u32[]{:S(2)}) %collective-permute-start.3) | collective-permute-done | bytes 1048608 | tf_op jit(solution)/shard_map/ppermute | solution.py:18
  172.7 20.7 %collective-permute-done.4 = f32[256,2,512]{2,0,1:T(8,128)} collective-permute-done((f32[256,2,512]{2,0,1:T(8,128)}, f32[256,2,512]{2,0,1:T(8,128)}, u32[]{:S(2)}, u32[]{:S(2)}) %collective-permute-start.4) | collective-permute-done | bytes 1048608 | tf_op jit(solution)/shard_map/ppermute | solution.py:18
  193.4 3.8 add_select_fusion.7
  197.2 42.6 %collective-permute-start.5 = (f32[256,2,512]{2,0,1:T(8,128)S(1)}, f32[256,2,512]{2,0,1:T(8,128)}, u32[]{:S(2)}, u32[]{:S(2)}) collective-permute-start(f32[256,2,512]{2,0,1:T(8,128)S(1)} %get-tuple-element.12), channel_id=1, source_target_pairs={{0,32},{32,0},{8,40},{40,8},{16,48},{48,16},{24,56},{56,24},{64,96... | collective-permute-start | bytes 3145736 | tf_op jit(solution)/shard_map/ppermute | solution.py:18
  240.0 68.9 %collective-permute-done.5 = f32[256,2,512]{2,0,1:T(8,128)} collective-permute-done((f32[256,2,512]{2,0,1:T(8,128)S(1)}, f32[256,2,512]{2,0,1:T(8,128)}, u32[]{:S(2)}, u32[]{:S(2)}) %collective-permute-start.5) | collective-permute-done | bytes 1048608 | tf_op jit(solution)/shard_map/ppermute | solution.py:18
  308.9 21.3 %collective-permute-done.6 = f32[256,2,512]{2,0,1:T(8,128)} collective-permute-done((f32[256,2,512]{2,0,1:T(8,128)}, f32[256,2,512]{2,0,1:T(8,128)}, u32[]{:S(2)}, u32[]{:S(2)}) %collective-permute-start.6) | collective-permute-done | bytes 1048608 | tf_op jit(solution)/shard_map/ppermute | solution.py:18
  330.2 3.7 add_select_fusion.5
  336.1 24.1 %collective-permute-done.7 = f32[256,2,512]{2,0,1:T(8,128)S(1)} collective-permute-done((f32[256,2,512]{2,0,1:T(8,128)}, f32[256,2,512]{2,0,1:T(8,128)S(1)}, u32[]{:S(2)}, u32[]{:S(2)}) %collective-permute-start.7) | collective-permute-done | bytes 1048608 | tf_op jit(solution)/shard_map/ppermute | solution.py:18
  361.2 19.6 %collective-permute-done.8 = f32[256,2,512]{2,0,1:T(8,128)} collective-permute-done((f32[256,2,512]{2,0,1:T(8,128)}, f32[256,2,512]{2,0,1:T(8,128)}, u32[]{:S(2)}, u32[]{:S(2)}) %collective-permute-start.8) | collective-permute-done | bytes 1048608 | tf_op jit(solution)/shard_map/ppermute | solution.py:18
  380.7 3.8 add_select_fusion.3
  385.4 2.1 collective-permute-done.10
  388.8 3.3 multiply_add_fusion
  394.9 3.0 fusion.30
  398.0 2.5 copy.8
  400.5 4.4 fusion.32
  404.9 3.0 convolution_subtract_fusion
  407.9 3.1 reshape.163
  411.0 4.2 convolution_add_fusion
  415.3 3.2 reshape.162
  418.4 1.7 multiply_subtract_fusion.2
  420.2 12.0 %fusion.28 = f32[256,512]{1,0:T(8,128)S(1)} fusion(f32[256,512]{1,0:T(8,128)S(1)} %bitcast.39), kind=kOutput, calls=%fused_computation.71 | convolution fusion | flops 403570688 | bytes 1048576 | tf_op jit(solution)/shard_map/dot_general | solution.py:36
  432.3 2.4 fusion.26
  434.7 1.6 convolution_subtract_fusion.1
  437.4 2.1 copy.11
  439.4 2.7 convolution_add_fusion.1
  446.8 1.8 collective-permute-start.13
  448.9 12.7 %collective-permute-done.13 = f32[256,2,256]{2,0,1:T(8,128)S(1)} collective-permute-done((f32[256,2,256]{2,0,1:T(8,128)S(1)}, f32[256,2,256]{2,0,1:T(8,128)S(1)}, u32[]{:S(2)}, u32[]{:S(2)}) %collective-permute-start.13) | collective-permute-done | bytes 524320 | tf_op jit(solution)/shard_map/ppermute | solution.py:18
  461.6 10.4 %collective-permute-done.14 = f32[256,2,256]{2,0,1:T(8,128)S(1)} collective-permute-done((f32[256,2,256]{2,0,1:T(8,128)S(1)}, f32[256,2,256]{2,0,1:T(8,128)S(1)}, u32[]{:S(2)}, u32[]{:S(2)}) %collective-permute-start.14) | collective-permute-done | bytes 524320 | tf_op jit(solution)/shard_map/ppermute | solution.py:18
  472.4 3.5 collective-permute-start.16
  475.9 35.1 %collective-permute-done.16 = f32[256,2,256]{2,0,1:T(8,128)S(1)} collective-permute-done((f32[256,2,256]{2,0,1:T(8,128)S(1)}, f32[256,2,256]{2,0,1:T(8,128)S(1)}, u32[]{:S(2)}, u32[]{:S(2)}) %collective-permute-start.16) | collective-permute-done | bytes 524320 | tf_op jit(solution)/shard_map/ppermute | solution.py:18
  511.0 9.9 %collective-permute-done.15 = f32[256,2,256]{2,0,1:T(8,128)S(1)} collective-permute-done((f32[256,2,256]{2,0,1:T(8,128)S(1)}, f32[256,2,256]{2,0,1:T(8,128)S(1)}, u32[]{:S(2)}, u32[]{:S(2)}) %collective-permute-start.15) | collective-permute-done | bytes 524320 | tf_op jit(solution)/shard_map/ppermute | solution.py:18
  521.2 3.1 collective-permute-start.17
  524.3 2.9 collective-permute-start.18
  527.3 32.8 %collective-permute-done.17 = f32[256,2,256]{2,0,1:T(8,128)S(1)} collective-permute-done((f32[256,2,256]{2,0,1:T(8,128)S(1)}, f32[256,2,256]{2,0,1:T(8,128)S(1)}, u32[]{:S(2)}, u32[]{:S(2)}) %collective-permute-start.17) | collective-permute-done | bytes 524320 | tf_op jit(solution)/shard_map/ppermute | solution.py:18
  560.0 11.1 %collective-permute-done.18 = f32[256,2,256]{2,0,1:T(8,128)S(1)} collective-permute-done((f32[256,2,256]{2,0,1:T(8,128)S(1)}, f32[256,2,256]{2,0,1:T(8,128)S(1)}, u32[]{:S(2)}, u32[]{:S(2)}) %collective-permute-start.18) | collective-permute-done | bytes 524320 | tf_op jit(solution)/shard_map/ppermute | solution.py:18
  571.6 2.0 collective-permute-start.20
  573.6 12.8 %collective-permute-done.19 = f32[256,2,256]{2,0,1:T(8,128)S(1)} collective-permute-done((f32[256,2,256]{2,0,1:T(8,128)S(1)}, f32[256,2,256]{2,0,1:T(8,128)S(1)}, u32[]{:S(2)}, u32[]{:S(2)}) %collective-permute-start.19) | collective-permute-done | bytes 524320 | tf_op jit(solution)/shard_map/ppermute | solution.py:18
  586.4 10.3 %collective-permute-done.20 = f32[256,2,256]{2,0,1:T(8,128)S(1)} collective-permute-done((f32[256,2,256]{2,0,1:T(8,128)S(1)}, f32[256,2,256]{2,0,1:T(8,128)S(1)}, u32[]{:S(2)}, u32[]{:S(2)}) %collective-permute-start.20) | collective-permute-done | bytes 524320 | tf_op jit(solution)/shard_map/ppermute | solution.py:18
  597.7 50.8 %all-gather.5.cloned.1.call-done = bf16[256,2048]{1,0:T(8,128)(2,1)} async-done(((bf16[256,256]{1,0:T(8,128)(2,1)}), bf16[256,2048]{1,0:T(8,128)(2,1)}) %all-gather.5.cloned.1.call-update) | async-done | bytes 1048592 | tf_op jit(solution)/shard_map/all_gather | solution.py:140
  648.5 2.6 convolution_convert_fusion
  (73 shorter events, 25.0 us)
Async XLA Ops:
  6.5 641.9 %copy-start = (bf16[2048,512]{1,0:T(8,128)(2,1)S(1)}, bf16[2048,512]{1,0:T(8,128)(2,1)}, u32[]{:S(2)}) copy-start(bf16[2048,512]{1,0:T(8,128)(2,1)} %param.11) | copy-start | bytes 6291460
  6.5 68.6 %all-gather.3.cloned.1.call-start = ((), (), s32[]{:S(2)}) async-start(), calls=%async_computation | async-start | bytes 2359296 | tf_op jit(solution)/shard_map/all_gather | solution.py:124
  7.3 641.2 %all-gather.5.cloned.1.call-start = ((), (), s32[]{:S(2)}) async-start(), calls=%async_computation.1 | async-start | bytes 1179648 | tf_op jit(solution)/shard_map/all_gather | solution.py:140
  75.1 6.7 %copy-start.10 = (f32[3,3,256]{2,1,0:T(4,128)S(1)}, f32[3,3,256]{2,1,0:T(4,128)}, u32[]{:S(2)}) copy-start(f32[3,3,256]{2,1,0:T(4,128)} %param.8) | copy-start | bytes 27652
  80.4 2.6 copy-start.9
  80.4 2.2 collective-permute-start
  82.9 0.9 copy-start.2
  83.8 0.8 copy-start.4
  85.6 29.9 %collective-permute-start.1 = (f32[256,2,512]{2,0,1:T(8,128)}, f32[256,2,512]{2,0,1:T(8,128)}, u32[]{:S(2)}, u32[]{:S(2)}) collective-permute-start(f32[256,2,512]{2,0,1:T(8,128)} %pad_maximum_fusion), channel_id=1, source_target_pairs={{0,128},{128,0},{8,136},{136,8},{16,144},{144,16},{24,152},{152,24... | collective-permute-start | bytes 3145736 | tf_op jit(solution)/shard_map/ppermute | solution.py:18
  92.3 43.4 %collective-permute-start.2 = (f32[256,2,512]{2,0,1:T(8,128)}, f32[256,2,512]{2,0,1:T(8,128)}, u32[]{:S(2)}, u32[]{:S(2)}) collective-permute-start(f32[256,2,512]{2,0,1:T(8,128)} %stack.13), channel_id=1, source_target_pairs={{0,128},{128,0},{8,136},{136,8},{16,144},{144,16},{24,152},{152,24... | collective-permute-start | bytes 3145736 | tf_op jit(solution)/shard_map/ppermute | solution.py:18
  139.2 32.5 %collective-permute-start.3 = (f32[256,2,512]{2,0,1:T(8,128)}, f32[256,2,512]{2,0,1:T(8,128)S(1)}, u32[]{:S(2)}, u32[]{:S(2)}) collective-permute-start(f32[256,2,512]{2,0,1:T(8,128)} %get-tuple-element.14), channel_id=1, source_target_pairs={{0,64},{64,0},{8,72},{72,8},{16,80},{80,16},{24,88},{88,24},{32,96... | collective-permute-start | bytes 3145736 | tf_op jit(solution)/shard_map/ppermute | solution.py:18
  144.0 49.4 %collective-permute-start.4 = (f32[256,2,512]{2,0,1:T(8,128)}, f32[256,2,512]{2,0,1:T(8,128)}, u32[]{:S(2)}, u32[]{:S(2)}) collective-permute-start(f32[256,2,512]{2,0,1:T(8,128)} %get-tuple-element.15), channel_id=1, source_target_pairs={{0,64},{64,0},{8,72},{72,8},{16,80},{80,16},{24,88},{88,24},{32,96... | collective-permute-start | bytes 3145736 | tf_op jit(solution)/shard_map/ppermute | solution.py:18
  171.7 1.0 copy-start.7
  197.2 111.7 %collective-permute-start.5 = (f32[256,2,512]{2,0,1:T(8,128)S(1)}, f32[256,2,512]{2,0,1:T(8,128)}, u32[]{:S(2)}, u32[]{:S(2)}) collective-permute-start(f32[256,2,512]{2,0,1:T(8,128)S(1)} %get-tuple-element.12), channel_id=1, source_target_pairs={{0,32},{32,0},{8,40},{40,8},{16,48},{48,16},{24,56},{56,24},{64,96... | collective-permute-start | bytes 3145736 | tf_op jit(solution)/shard_map/ppermute | solution.py:18
  239.8 90.4 %collective-permute-start.6 = (f32[256,2,512]{2,0,1:T(8,128)}, f32[256,2,512]{2,0,1:T(8,128)}, u32[]{:S(2)}, u32[]{:S(2)}) collective-permute-start(f32[256,2,512]{2,0,1:T(8,128)} %get-tuple-element.13), channel_id=1, source_target_pairs={{0,32},{32,0},{8,40},{40,8},{16,48},{48,16},{24,56},{56,24},{64,96... | collective-permute-start | bytes 3145736 | tf_op jit(solution)/shard_map/ppermute | solution.py:18
  333.9 26.3 %collective-permute-start.7 = (f32[256,2,512]{2,0,1:T(8,128)}, f32[256,2,512]{2,0,1:T(8,128)S(1)}, u32[]{:S(2)}, u32[]{:S(2)}) collective-permute-start(f32[256,2,512]{2,0,1:T(8,128)} %get-tuple-element.10), channel_id=1, source_target_pairs={{0,16},{16,0},{8,24},{24,8},{32,48},{48,32},{40,56},{56,40},{64,80... | collective-permute-start | bytes 3145736 | tf_op jit(solution)/shard_map/ppermute | solution.py:18
  334.6 46.1 %collective-permute-start.8 = (f32[256,2,512]{2,0,1:T(8,128)}, f32[256,2,512]{2,0,1:T(8,128)}, u32[]{:S(2)}, u32[]{:S(2)}) collective-permute-start(f32[256,2,512]{2,0,1:T(8,128)} %get-tuple-element.11), channel_id=1, source_target_pairs={{0,16},{16,0},{8,24},{24,8},{32,48},{48,32},{40,56},{56,40},{64,80... | collective-permute-start | bytes 3145736 | tf_op jit(solution)/shard_map/ppermute | solution.py:18
  360.2 1.0 copy-start.8
  384.5 3.0 collective-permute-start.10
  384.5 4.3 collective-permute-start.9
  400.5 4.4 copy-start.1
  400.5 4.4 copy-start.6
  415.3 3.2 copy-start.5
  443.8 2.0 collective-permute-start.12
  444.0 2.5 collective-permute-start.11
  446.8 14.9 %collective-permute-start.13 = (f32[256,2,256]{2,0,1:T(8,128)S(1)}, f32[256,2,256]{2,0,1:T(8,128)S(1)}, u32[]{:S(2)}, u32[]{:S(2)}) collective-permute-start(f32[256,2,256]{2,0,1:T(8,128)S(1)} %get-tuple-element.22), channel_id=1, source_target_pairs={{0,16},{16,0},{8,24},{24,8},{32,48},{48,32},{40,56},{56,40},{64,80... | collective-permute-start | bytes 1572872 | tf_op jit(solution)/shard_map/ppermute | solution.py:18
  448.6 23.5 %collective-permute-start.14 = (f32[256,2,256]{2,0,1:T(8,128)S(1)}, f32[256,2,256]{2,0,1:T(8,128)S(1)}, u32[]{:S(2)}, u32[]{:S(2)}) collective-permute-start(f32[256,2,256]{2,0,1:T(8,128)S(1)} %get-tuple-element.23), channel_id=1, source_target_pairs={{0,16},{16,0},{8,24},{24,8},{32,48},{48,32},{40,56},{56,40},{64,80... | collective-permute-start | bytes 1572872 | tf_op jit(solution)/shard_map/ppermute | solution.py:18
  472.4 38.7 %collective-permute-start.16 = (f32[256,2,256]{2,0,1:T(8,128)S(1)}, f32[256,2,256]{2,0,1:T(8,128)S(1)}, u32[]{:S(2)}, u32[]{:S(2)}) collective-permute-start(f32[256,2,256]{2,0,1:T(8,128)S(1)} %get-tuple-element.20), channel_id=1, source_target_pairs={{0,32},{32,0},{8,40},{40,8},{16,48},{48,16},{24,56},{56,24},{64,96... | collective-permute-start | bytes 1572872 | tf_op jit(solution)/shard_map/ppermute | solution.py:18
  475.8 45.1 %collective-permute-start.15 = (f32[256,2,256]{2,0,1:T(8,128)S(1)}, f32[256,2,256]{2,0,1:T(8,128)S(1)}, u32[]{:S(2)}, u32[]{:S(2)}) collective-permute-start(f32[256,2,256]{2,0,1:T(8,128)S(1)} %get-tuple-element.21), channel_id=1, source_target_pairs={{0,32},{32,0},{8,40},{40,8},{16,48},{48,16},{24,56},{56,24},{64,96... | collective-permute-start | bytes 1572872 | tf_op jit(solution)/shard_map/ppermute | solution.py:18
  521.2 38.8 %collective-permute-start.17 = (f32[256,2,256]{2,0,1:T(8,128)S(1)}, f32[256,2,256]{2,0,1:T(8,128)S(1)}, u32[]{:S(2)}, u32[]{:S(2)}) collective-permute-start(f32[256,2,256]{2,0,1:T(8,128)S(1)} %get-tuple-element.18), channel_id=1, source_target_pairs={{0,64},{64,0},{8,72},{72,8},{16,80},{80,16},{24,88},{88,24},{32,96... | collective-permute-start | bytes 1572872 | tf_op jit(solution)/shard_map/ppermute | solution.py:18
  524.3 46.8 %collective-permute-start.18 = (f32[256,2,256]{2,0,1:T(8,128)S(1)}, f32[256,2,256]{2,0,1:T(8,128)S(1)}, u32[]{:S(2)}, u32[]{:S(2)}) collective-permute-start(f32[256,2,256]{2,0,1:T(8,128)S(1)} %get-tuple-element.19), channel_id=1, source_target_pairs={{0,64},{64,0},{8,72},{72,8},{16,80},{80,16},{24,88},{88,24},{32,96... | collective-permute-start | bytes 1572872 | tf_op jit(solution)/shard_map/ppermute | solution.py:18
  571.5 25.4 %copy-start.3 = (f32[256,768]{1,0:T(8,128)S(1)}, f32[256,768]{1,0:T(8,128)}, u32[]{:S(2)}) copy-start(f32[256,768]{1,0:T(8,128)} %copy-done.2) | copy-start | bytes 2359300
  571.5 25.4 %copy-start.11 = (f32[256]{0:T(256)S(1)}, f32[256]{0:T(256)}, u32[]{:S(2)}) copy-start(f32[256]{0:T(256)} %param.10) | copy-start | bytes 3076
  571.5 14.9 %collective-permute-start.19 = (f32[256,2,256]{2,0,1:T(8,128)S(1)}, f32[256,2,256]{2,0,1:T(8,128)S(1)}, u32[]{:S(2)}, u32[]{:S(2)}) collective-permute-start(f32[256,2,256]{2,0,1:T(8,128)S(1)} %get-tuple-element.17), channel_id=1, source_target_pairs={{0,128},{128,0},{8,136},{136,8},{16,144},{144,16},{24,152},{152,24... | collective-permute-start | bytes 1572872 | tf_op jit(solution)/shard_map/ppermute | solution.py:18
  571.6 25.1 %collective-permute-start.20 = (f32[256,2,256]{2,0,1:T(8,128)S(1)}, f32[256,2,256]{2,0,1:T(8,128)S(1)}, u32[]{:S(2)}, u32[]{:S(2)}) collective-permute-start(f32[256,2,256]{2,0,1:T(8,128)S(1)} %get-tuple-element.16), channel_id=1, source_target_pairs={{0,128},{128,0},{8,136},{136,8},{16,144},{144,16},{24,152},{152,24... | collective-permute-start | bytes 1572872 | tf_op jit(solution)/shard_map/ppermute | solution.py:18
Sparse Core Ops, SparseCore 0:
  9.8 65.2 all-gather.2
  597.8 50.5 all-gather.4
where the time goes:
time: 662 us; the launch traced here: 658 us
  waiting for transfers between devices  476 us (72%)
  starting transfers between devices  72.8 us (11%)
  matrix products  41.3 us (6%)
  local copies, waits for them, and re-layouts  27 us (4%)
  other arithmetic  26 us (4%)
  between operations  14.7 us (2%)
    ppermute x20, waiting for transfers between devices, from_partner(): return lax.ppermute(block, axis, route)  365 us
    ppermute x20, starting transfers between devices, from_partner(): return lax.ppermute(block, axis, route)  71.3 us
    all_gather x1, waiting for transfers between devices, shards(): lax.all_gather(inputs, 'ch', axis=1, tiled=True)  59.2 us
    all_gather x1, waiting for transfers between devices, shards(): lax.all_gather(gated_out, 'ch', axis=1, tiled=True)  50.8 us
    dot_general x2, matrix products, row_transform(): jnp.dot(cosine, left, precision=HIGH, preferred_element_type=jnp.float32)  16.4 us
    select_n x4, other arithmetic, forward_butterfly(): real_part = jnp.where(upper, turned_real, real_part + other_real)  14.7 us
  transfers between devices with their start and end apart: 23, of which 23 were waited for; matrix products, arithmetic and copies ran while one was open for 1% of the time, Pallas kernels for 0%

commit v1 on v0

v1 whole, which is shorter than its diff:
```python
import functools
import math

import jax
import jax.numpy as jnp
import ml_dtypes
import numpy as np
from jax import lax
from jax.experimental import pallas as pl
from jax.experimental.pallas import tpu as pltpu
from jax.sharding import PartitionSpec as P

MESH = pl.DeviceIdType.MESH
BF16 = jnp.bfloat16
F32 = jnp.float32
LANES = 128
OWN = 8


def halves(table):
    high = table.astype(ml_dtypes.bfloat16)
    low = (table - high.astype(np.float64)).astype(ml_dtypes.bfloat16)
    return np.stack([high, low])


def tables(length):
    rows = length // LANES
    k1 = np.arange(rows)[:, None] + 0.5
    n1 = np.arange(rows)[None, :]
    n2 = np.arange(LANES)[None, :]
    k2 = np.arange(LANES)[:, None]
    outer = 2.0 * math.pi * k1 * n1 / (2 * rows)
    first = np.concatenate([np.cos(outer), -np.sin(outer)], 0)
    turn = 2.0 * math.pi * k1 * n2 / (2 * length)
    twist = np.stack([np.cos(turn), -np.sin(turn)]).astype(np.float32)
    inner = 2.0 * math.pi * k2 * n2 / LANES
    cosine, sine = np.cos(inner), np.sin(inner)
    second = np.block([[cosine, -sine], [sine, cosine]])
    back = np.block([[cosine, sine], [-sine, cosine]])
    return (
        halves(first),
        halves(first.T / length),
        np.concatenate([halves(second), halves(back)]),
        twist,
    )


def split(value):
    high = value.astype(BF16)
    return high, (value - high.astype(F32)).astype(BF16)


def dot(left, right):
    return jnp.dot(left, right, preferred_element_type=F32)


def kernel(nctx, nch, ny, *refs):
    (
        x_hbm, w_hbm, taps_hbm, filt_hbm, skip_hbm, wo_hbm,
        first_hbm, last_hbm, mid_hbm, twist_hbm,
        out_ref,
        xg, w, taps, filt, skip, wo, first, last, mid, twist,
        proj, gate, gated, hsend, hrecv, gsend, grecv, csend, crecv, yg,
        line, spec, hspec, dhi, dlo, acc,
        local_sem, x_send, x_recv, halo_sem, h_sem, g_sem, c_sem, y_send, y_recv,
    ) = refs
    ctx = lax.axis_index("ctx")
    ch = lax.axis_index("ch")
    rows, feats = x_hbm.shape
    chans = filt_hbm.shape[1]
    k1 = first_hbm.shape[2]

    def peer(step):
        nx = nch // ny
        dx = (step // ny) % nx
        dx = dx ^ (dx // 2)
        dy = step % ny
        x, y = ch // ny, ch % ny
        yy = (y + dy) % ny
        return ((x + dx) % nx) * ny + yy, ((x + nx - dx) % nx) * ny + yy

    def loads():
        pairs = (
            (x_hbm, xg.at[ch]), (filt_hbm, filt), (first_hbm, first), (mid_hbm, mid), (twist_hbm, twist),
            (last_hbm, last), (taps_hbm, taps), (skip_hbm, skip), (w_hbm, w), (wo_hbm, wo),
        )
        return [pltpu.make_async_copy(s, d, local_sem.at[i]) for i, (s, d) in enumerate(pairs)]

    local = loads()
    for copy in local:
        copy.start()

    barrier = pltpu.get_barrier_semaphore()

    def greet_ctx(d, carry):
        pl.semaphore_signal(barrier, inc=1, device_id={"ctx": (ctx + d) % nctx}, device_id_type=MESH)
        return carry

    def greet_ch(d, carry):
        pl.semaphore_signal(barrier, inc=1, device_id={"ch": (ch + d) % nch}, device_id_type=MESH)
        return carry

    lax.fori_loop(1, nch, greet_ch, 0)
    lax.fori_loop(1, nctx, greet_ctx, 0)
    pl.semaphore_wait(barrier, nctx + nch - 2)


    def gather(source, slots, send, recv, step):
        to, _ = peer(step)
        return pltpu.make_async_remote_copy(
            src_ref=source, dst_ref=slots.at[ch], send_sem=send.at[step], recv_sem=recv.at[step],
            device_id={"ch": to}, device_id_type=MESH,
        )

    def x_start(step, carry):
        gather(x_hbm, xg, x_send, x_recv, step).start()
        return carry

    lax.fori_loop(1, nch, x_start, 0)


    def exchange(send, recv, sem):
        def body(d, carry):
            to = (ctx + d) % nctx
            pltpu.make_async_remote_copy(
                src_ref=send.at[to], dst_ref=recv.at[ctx], send_sem=sem.at[0], recv_sem=sem.at[1],
                device_id={"ctx": to}, device_id_type=MESH,
            ).start()
            return carry

        lax.fori_loop(1, nctx, body, 0)
        recv[pl.ds(ctx, 1)] = send[pl.ds(ctx, 1)]

    def whole(send, sem):
        part = send.at[pl.ds(0, nctx - 1)]
        return pltpu.make_async_copy(part, part, sem)

    def to_parts(block):
        turned = block.T.reshape(nctx, OWN, rows)
        return jnp.concatenate([turned[:, :, :LANES], turned[:, :, LANES:]], axis=1)

    def forward(result, exact):
        block = jnp.concatenate([line[pl.ds(c, k1, stride=OWN), :] for c in range(OWN)], axis=1)
        high, low = split(block)
        turned = dot(first[0], high) + dot(first[1], high)
        if not exact:
            turned = turned + dot(first[0], low)
        for c in range(OWN):
            real = turned[:k1, c * LANES : (c + 1) * LANES]
            imag = turned[k1:, c * LANES : (c + 1) * LANES]
            at = pl.ds(c * k1, k1)
            dhi[at, :LANES], dlo[at, :LANES] = split(real * twist[0] - imag * twist[1])
            dhi[at, LANES:], dlo[at, LANES:] = split(real * twist[1] + imag * twist[0])
        result[...] = dot(dhi[...], mid[0]) + dot(dhi[...], mid[1]) + dot(dlo[...], mid[0])

    def backward():
        xr, xi = spec[:, :LANES], spec[:, LANES:]
        hr, hi = hspec[:, :LANES], hspec[:, LANES:]
        dhi[:, :LANES], dlo[:, :LANES] = split(xr * hr - xi * hi)
        dhi[:, LANES:], dlo[:, LANES:] = split(xr * hi + xi * hr)
        spec[...] = dot(dhi[...], mid[2]) + dot(dhi[...], mid[3]) + dot(dlo[...], mid[2])
        cols = []
        for c in range(OWN):
            at = pl.ds(c * k1, k1)
            real, imag = spec[at, :LANES], spec[at, LANES:]
            cols.append(
                jnp.concatenate([real * twist[0] + imag * twist[1], imag * twist[0] - real * twist[1]], axis=0)
            )
        high, low = split(jnp.concatenate(cols, axis=1))
        signal = dot(last[0], high) + dot(last[1], high) + dot(last[0], low)
        for c in range(OWN):
            line[pl.ds(c, k1, stride=OWN), :] = signal[:, c * LANES : (c + 1) * LANES]

    for copy in local[1:6]:
        copy.wait()
    hsend[...] = to_parts(filt[...])
    exchange(hsend, hrecv, h_sem)
    whole(hsend, h_sem.at[1]).wait()
    line[...] = hrecv[...].reshape(line.shape)
    forward(hspec, False)
    whole(hsend, h_sem.at[0]).wait()

    for copy in local[6:] + local[:1]:
        copy.wait()
    top = 8

    def project(step, carry):
        _, src = peer(step)

        @pl.when(step > 0)
        def _():
            pltpu.make_async_remote_copy(
                src_ref=x_hbm, dst_ref=xg.at[src], send_sem=x_send.at[step], recv_sem=x_recv.at[step],
                device_id={"ch": src}, device_id_type=MESH,
            ).wait_recv()

        part = xg[src]
        at = pl.ds(pl.multiple_of(src * feats, feats), feats)
        for s in range(3):
            cols = pl.ds(s * chans, chans)
            proj[top:, cols] += dot(part, w[s, at, :])
        return carry

    proj[top:] = jnp.zeros((rows, 3 * chans), F32)
    lax.fori_loop(0, nch, project, 0)
    halo = pltpu.make_async_remote_copy(
        src_ref=proj.at[pl.ds(rows, top)], dst_ref=proj.at[pl.ds(0, top)],
        send_sem=halo_sem.at[0], recv_sem=halo_sem.at[1],
        device_id={"ctx": (ctx + 1) % nctx}, device_id_type=MESH,
    )
    halo.start()
    halo.wait()
    proj[:top] = jnp.where(ctx == 0, 0.0, proj[:top])

    def stream(s):
        cols = pl.ds(s * chans, chans)
        return (
            taps[0, s : s + 1, :] * proj[top:, cols]
            + taps[1, s : s + 1, :] * proj[pl.ds(top - 1, rows), cols]
            + taps[2, s : s + 1, :] * proj[pl.ds(top - 2, rows), cols]
        )

    gated[...] = stream(0) * stream(2)
    gsend[...] = to_parts(gated[...]).astype(BF16)
    exchange(gsend, grecv, g_sem)
    gate[...] = stream(1)
    whole(gsend, g_sem.at[1]).wait()

    line[...] = grecv[...].astype(F32).reshape(line.shape)
    forward(spec, True)
    backward()
    csend[...] = line[...].reshape(csend.shape).astype(BF16)
    exchange(csend, crecv, c_sem)
    whole(csend, c_sem.at[1]).wait()
    back = crecv[...].astype(F32)
    for part in range(2):
        at = pl.ds(part * LANES, LANES)
        conv = back[:, part * OWN : (part + 1) * OWN, :].reshape(chans, LANES).T
        mixed = gate[at, :] * (conv + skip[...] * gated[at, :])
        yg[ch, at, :] = mixed.astype(BF16)

    def y_start(step, carry):
        gather(yg.at[ch], yg, y_send, y_recv, step).start()
        return carry

    lax.fori_loop(1, nch, y_start, 0)

    def mix(step, carry):
        _, src = peer(step)

        @pl.when(step > 0)
        def _():
            pltpu.make_async_remote_copy(
                src_ref=yg.at[ch], dst_ref=yg.at[src], send_sem=y_send.at[step], recv_sem=y_recv.at[step],
                device_id={"ch": src}, device_id_type=MESH,
            ).wait_recv()

        at = pl.ds(pl.multiple_of(src * chans, chans), chans)
        acc[...] += dot(yg[src], wo[at, :])
        return carry

    acc[...] = jnp.zeros_like(acc)
    lax.fori_loop(0, nch, mix, 0)
    out_ref[...] = acc[...].astype(BF16)

    def drain(step, carry):
        gather(x_hbm, xg, x_send, x_recv, step).wait_send()
        gather(yg.at[ch], yg, y_send, y_recv, step).wait_send()
        return carry

    lax.fori_loop(1, nch, drain, 0)
    whole(gsend, g_sem.at[0]).wait()
    whole(csend, c_sem.at[0]).wait()


def shards(nctx, nch, inputs, in_weight, short_kernel, long_filter, skip_gain, out_weight):
    rows, feats = inputs.shape
    width, _, chans = in_weight.shape
    mixed = out_weight.shape[1]
    length = rows * nctx
    consts = [jnp.asarray(t) for t in tables(length)]
    k1 = length // LANES
    operands = [
        inputs, jnp.transpose(in_weight, (1, 0, 2)), short_kernel, long_filter,
        skip_gain.reshape(1, chans), out_weight, *consts,
    ]
    vm = pltpu.VMEM
    parts = (nctx, 2 * OWN, LANES)
    scratch = [
        vm((nch, rows, feats), BF16), vm((3, width, chans), BF16), vm(short_kernel.shape, F32),
        vm((rows, chans), F32), vm((1, chans), F32), vm(out_weight.shape, BF16),
        *[vm(c.shape, c.dtype) for c in consts],
        vm((rows + 8, 3 * chans), F32), vm((rows, chans), F32), vm((rows, chans), F32),
        vm(parts, F32), vm(parts, F32), vm(parts, BF16), vm(parts, BF16), vm(parts, BF16), vm(parts, BF16),
        vm((nch, rows, chans), BF16),
        vm((k1 * OWN, LANES), F32), vm((k1 * OWN, 2 * LANES), F32), vm((k1 * OWN, 2 * LANES), F32),
        vm((k1 * OWN, 2 * LANES), BF16), vm((k1 * OWN, 2 * LANES), BF16), vm((rows, mixed), F32),
    ]
    dma = pltpu.SemaphoreType.DMA
    sems = [dma((10,)), dma((nch,)), dma((nch,)), dma((2,)), dma((2,)), dma((2,)), dma((2,)), dma((nch,)), dma((nch,))]
    return pl.pallas_call(
        functools.partial(kernel, nctx, nch, 2),
        out_shape=jax.ShapeDtypeStruct((rows, mixed), BF16),
        in_specs=[pl.BlockSpec(memory_space=pl.ANY)] * len(operands),
        out_specs=pl.BlockSpec(memory_space=pltpu.VMEM),
        scratch_shapes=scratch + sems,
        compiler_params=pltpu.CompilerParams(
            collective_id=0, has_side_effects=True, vmem_limit_bytes=40 * 1024 * 1024
        ),
    )(*operands)


def solution(mesh):
    placed = (
        P("ctx", "ch"),
        P(None, None, "ch"),
        P(None, None, "ch"),
        P("ctx", "ch"),
        P("ch"),
        P(None, "ch"),
    )
    body = functools.partial(shards, mesh.shape["ctx"], mesh.shape["ch"])
    return jax.shard_map(body, mesh=mesh, in_specs=placed, out_specs=P("ctx", "ch"), check_vma=False)
```

time: 662 us -> 88.6 us (0.13)
  the two profiles are of different devices: /device:TPU:6 before, /device:TPU:16 now
where the time goes in v1:
time: 88.6 us; the launch traced here: 88.1 us
  Pallas kernels  76.2 us (86%)
  local copies, waits for them, and re-layouts  11.8 us (13%)
    pallas_call x1, Pallas kernels, shards(): pl.pallas_call(functools.partial(kernel, nctx, nch, 2), out_shape=jax.Sha...  76.2 us
    unnamed x21, local copies, waits for them, and re-layouts  11.8 us

profile of v1, /device:TPU:16, one launch (start us, length us, event | category | flops | bytes accessed | tf_op | source)
XLA Modules:
  0.0 88.1 jit_solution(4018662618123036517)
XLA Ops:
  0.0 0.0 copy-start
  0.0 2.8 %copy-done = bf16[4096,3,256]{2,0,1:T(8,128)(2,1)S(1)} copy-done((bf16[4096,3,256]{2,0,1:T(8,128)(2,1)S(1)}, bf16[4096,3,256]{2,0,1:T(8,128)(2,1)}, u32[]{:S(2)}) %copy-start) | copy-done | bytes 6291480
  2.8 0.0 copy-start.1
  2.8 1.6 %copy-done.1 = bf16[2048,512]{1,0:T(8,128)(2,1)S(1)} copy-done((bf16[2048,512]{1,0:T(8,128)(2,1)S(1)}, bf16[2048,512]{1,0:T(8,128)(2,1)}, u32[]{:S(2)}) %copy-start.1) | copy-done | bytes 2097176
  4.4 0.0 copy-start.2
  4.4 1.0 %copy-done.2 = bf16[4,256,256]{2,1,0:T(8,128)(2,1)S(1)} copy-done((bf16[4,256,256]{2,1,0:T(8,128)(2,1)S(1)}, bf16[4,256,256]{2,1,0:T(8,128)(2,1)}, u32[]{:S(2)}) %copy-start.2) | copy-done | bytes 524312
  5.4 0.0 copy-start.3
  5.4 0.9 %copy-done.3 = bf16[256,512]{1,0:T(8,128)(2,1)S(1)} copy-done((bf16[256,512]{1,0:T(8,128)(2,1)S(1)}, bf16[256,512]{1,0:T(8,128)(2,1)}, u32[]{:S(2)}) %copy-start.3) | copy-done | bytes 262168
  6.4 0.0 copy-start.4
  6.4 0.9 %copy-done.4 = f32[256,256]{1,0:T(8,128)S(1)} copy-done((f32[256,256]{1,0:T(8,128)S(1)}, f32[256,256]{1,0:T(8,128)}, u32[]{:S(2)}) %copy-start.4) | copy-done | bytes 262168
  7.3 0.0 copy-start.5
  7.3 0.8 copy-done.5
  8.2 0.0 copy-start.6
  8.2 0.8 copy-done.6
  9.0 0.0 copy-start.7
  9.0 0.8 copy-done.7
  9.8 0.0 copy-start.8
  9.8 0.7 copy-done.8
  10.5 0.0 copy-start.9
  10.5 0.7 copy-done.9
  11.1 76.2 %shard_map.100 = bf16[256,512]{1,0:T(8,128)(2,1)S(1)} custom-call(bf16[256,512]{1,0:T(8,128)(2,1)S(1)} %copy-done.3, bf16[3,4096,256]{2,1,0:T(8,128)(2,1)S(1)} %bitcast.2, f32[3,3,256]{2,1,0:T(4,128)S(1)} %copy-done.8, f32[256,256]{1,0:T(8,128)S(1)} %copy-done.4, f32[1,256]{1,0:T(1,128)S(1)} %bitcast.3, bf16[2048,512]{1,0:T(8,128)(2,1)S(1)} %copy-done.1, ...), custom_call_target="tpu_custom_call" | custom-call | tf_op jit(solution)/shard_map/pallas_call | solution.py:301
  87.4 0.7 copy.12
Async XLA Ops:
  0.0 2.8 %copy-start = (bf16[4096,3,256]{2,0,1:T(8,128)(2,1)S(1)}, bf16[4096,3,256]{2,0,1:T(8,128)(2,1)}, u32[]{:S(2)}) copy-start(bf16[4096,3,256]{2,0,1:T(8,128)(2,1)} %param.11) | copy-start | bytes 18874372
  2.8 1.6 %copy-start.1 = (bf16[2048,512]{1,0:T(8,128)(2,1)S(1)}, bf16[2048,512]{1,0:T(8,128)(2,1)}, u32[]{:S(2)}) copy-start(bf16[2048,512]{1,0:T(8,128)(2,1)} %refs_5_.1) | copy-start | bytes 6291460
  4.4 1.0 %copy-start.2 = (bf16[4,256,256]{2,1,0:T(8,128)(2,1)S(1)}, bf16[4,256,256]{2,1,0:T(8,128)(2,1)}, u32[]{:S(2)}) copy-start(bf16[4,256,256]{2,1,0:T(8,128)(2,1)} %constant.10.clone.refs_8_) | copy-start | bytes 1572868
  5.4 0.9 %copy-start.3 = (bf16[256,512]{1,0:T(8,128)(2,1)S(1)}, bf16[256,512]{1,0:T(8,128)(2,1)}, u32[]{:S(2)}) copy-start(bf16[256,512]{1,0:T(8,128)(2,1)} %refs_0_.1) | copy-start | bytes 786436
  6.4 0.9 %copy-start.4 = (f32[256,256]{1,0:T(8,128)S(1)}, f32[256,256]{1,0:T(8,128)}, u32[]{:S(2)}) copy-start(f32[256,256]{1,0:T(8,128)} %refs_3_.1) | copy-start | bytes 786436
  7.3 0.8 copy-start.5
  8.2 0.8 copy-start.6
  9.0 0.8 copy-start.7
  9.8 0.7 copy-start.8
  10.5 0.7 copy-start.9

commit v2 on v1

--- a/solution.py
+++ b/solution.py
@@ -70,14 +70,14 @@
     chans = filt_hbm.shape[1]
     k1 = first_hbm.shape[2]
 
-    def peer(step):
-        nx = nch // ny
-        dx = (step // ny) % nx
-        dx = dx ^ (dx // 2)
-        dy = step % ny
-        x, y = ch // ny, ch % ny
-        yy = (y + dy) % ny
-        return ((x + dx) % nx) * ny + yy, ((x + nx - dx) % nx) * ny + yy
+    nx = nch // ny
+    half = rows // 2
+
+    def at_ch(dx, dy):
+        return ((ch // ny + dx) % nx) * ny + (ch % ny + dy) % ny
+
+    own, plus, minus, two = at_ch(0, 0), at_ch(1, 0), at_ch(nx - 1, 0), at_ch(2, 0)
+    own2, plus2, minus2, two2 = at_ch(0, 1), at_ch(1, 1), at_ch(nx - 1, 1), at_ch(2, 1)
 
     def loads():
         pairs = (
@@ -105,18 +105,51 @@
     pl.semaphore_wait(barrier, nctx + nch - 2)
 
 
-    def gather(source, slots, send, recv, step):
-        to, _ = peer(step)
-        return pltpu.make_async_remote_copy(
-            src_ref=source, dst_ref=slots.at[ch], send_sem=send.at[step], recv_sem=recv.at[step],
-            device_id={"ch": to}, device_id_type=MESH,
-        )
-
-    def x_start(step, carry):
-        gather(x_hbm, xg, x_send, x_recv, step).start()
-        return carry
-
-    lax.fori_loop(1, nch, x_start, 0)
+    def gather(source, slots, send, recv):
+        started = []
+
+        def piece(block, h):
+            return slots.at[block, pl.ds(h * half, half)]
+
+        def push(block, h, to, src=None):
+            copy = pltpu.make_async_remote_copy(
+                src_ref=piece(block, h) if src is None else src.at[pl.ds(h * half, half)],
+                dst_ref=piece(block, h), send_sem=send.at[len(started)], recv_sem=recv.at[block, h],
+                device_id={"ch": to}, device_id_type=MESH,
+            )
+            copy.start()
+            started.append(copy)
+
+        def pull(block, h):
+            pltpu.make_async_remote_copy(
+                src_ref=piece(block, h), dst_ref=piece(block, h), send_sem=send.at[0], recv_sem=recv.at[block, h],
+                device_id={"ch": own2}, device_id_type=MESH,
+            ).wait_recv()
+
+        def begin():
+            for h, to in ((0, own2), (0, plus), (1, minus), (1, own2), (1, plus), (0, minus)):
+                push(own, h, to, source)
+
+        def forward_first():
+            pull(own2, 0), push(own2, 0, plus)
+            pull(own2, 1), push(own2, 1, minus)
+            pull(minus, 0), push(minus, 0, plus)
+            pull(plus, 1), push(plus, 1, minus)
+            pull(minus, 1), push(minus, 1, own2)
+            pull(plus, 0), push(plus, 0, own2)
+
+        def forward_second():
+            pull(minus2, 0), push(minus2, 0, plus)
+            pull(plus2, 1), push(plus2, 1, minus)
+
+        def finish():
+            for copy in started:
+                copy.wait_send()
+
+        return begin, forward_first, forward_second, pull, finish
+
+    x_begin, x_first, x_second, x_pull, x_finish = gather(x_hbm, xg, x_send, x_recv)
+    x_begin()
 
 
     def exchange(send, recv, sem):
@@ -175,34 +208,31 @@
         copy.wait()
     hsend[...] = to_parts(filt[...])
     exchange(hsend, hrecv, h_sem)
+    for copy in local[6:] + local[:1]:
+        copy.wait()
+    top = 8
+
+    def project(block, first_one=False):
+        part = xg[block]
+        at = pl.ds(pl.multiple_of(block * feats, feats), feats)
+        for s in range(3):
+            cols = pl.ds(s * chans, chans)
+            term = dot(part, w[s, at, :])
+            proj[top:, cols] = term if first_one else proj[top:, cols] + term
+
+    project(own, True)
+    x_first()
+    for block in (own2, minus, plus):
+        project(block)
+
     whole(hsend, h_sem.at[1]).wait()
     line[...] = hrecv[...].reshape(line.shape)
     forward(hspec, False)
-    whole(hsend, h_sem.at[0]).wait()
-
-    for copy in local[6:] + local[:1]:
-        copy.wait()
-    top = 8
-
-    def project(step, carry):
-        _, src = peer(step)
-
-        @pl.when(step > 0)
-        def _():
-            pltpu.make_async_remote_copy(
-                src_ref=x_hbm, dst_ref=xg.at[src], send_sem=x_send.at[step], recv_sem=x_recv.at[step],
-                device_id={"ch": src}, device_id_type=MESH,
-            ).wait_recv()
-
-        part = xg[src]
-        at = pl.ds(pl.multiple_of(src * feats, feats), feats)
-        for s in range(3):
-            cols = pl.ds(s * chans, chans)
-            proj[top:, cols] += dot(part, w[s, at, :])
-        return carry
-
-    proj[top:] = jnp.zeros((rows, 3 * chans), F32)
-    lax.fori_loop(0, nch, project, 0)
+    x_second()
+    for block, waits in ((two, (0, 1)), (minus2, (1,)), (plus2, (0,)), (two2, (0, 1))):
+        for h in waits:
+            x_pull(block, h)
+        project(block)
     halo = pltpu.make_async_remote_copy(
         src_ref=proj.at[pl.ds(rows, top)], dst_ref=proj.at[pl.ds(0, top)],
         send_sem=halo_sem.at[0], recv_sem=halo_sem.at[1],
@@ -237,38 +267,29 @@
         at = pl.ds(part * LANES, LANES)
         conv = back[:, part * OWN : (part + 1) * OWN, :].reshape(chans, LANES).T
         mixed = gate[at, :] * (conv + skip[...] * gated[at, :])
-        yg[ch, at, :] = mixed.astype(BF16)
-
-    def y_start(step, carry):
-        gather(yg.at[ch], yg, y_send, y_recv, step).start()
-        return carry
-
-    lax.fori_loop(1, nch, y_start, 0)
-
-    def mix(step, carry):
-        _, src = peer(step)
-
-        @pl.when(step > 0)
-        def _():
-            pltpu.make_async_remote_copy(
-                src_ref=yg.at[ch], dst_ref=yg.at[src], send_sem=y_send.at[step], recv_sem=y_recv.at[step],
-                device_id={"ch": src}, device_id_type=MESH,
-            ).wait_recv()
-
-        at = pl.ds(pl.multiple_of(src * chans, chans), chans)
-        acc[...] += dot(yg[src], wo[at, :])
-        return carry
-
-    acc[...] = jnp.zeros_like(acc)
-    lax.fori_loop(0, nch, mix, 0)
+        yg[own, at, :] = mixed.astype(BF16)
+
+    y_begin, y_first, y_second, y_pull, y_finish = gather(yg.at[own], yg, y_send, y_recv)
+
+    def mix(block):
+        at = pl.ds(pl.multiple_of(block * chans, chans), chans)
+        return dot(yg[block], wo[at, :])
+
+    y_begin()
+    acc[...] = mix(own)
+    y_first()
+    for block in (own2, minus, plus):
+        acc[...] += mix(block)
+    y_second()
+    for block, waits in ((two, (0, 1)), (minus2, (1,)), (plus2, (0,)), (two2, (0, 1))):
+        for h in waits:
+            y_pull(block, h)
+        acc[...] += mix(block)
     out_ref[...] = acc[...].astype(BF16)
 
-    def drain(step, carry):
-        gather(x_hbm, xg, x_send, x_recv, step).wait_send()
-        gather(yg.at[ch], yg, y_send, y_recv, step).wait_send()
-        return carry
-
-    lax.fori_loop(1, nch, drain, 0)
+    x_finish()
+    y_finish()
+    whole(hsend, h_sem.at[0]).wait()
     whole(gsend, g_sem.at[0]).wait()
     whole(csend, c_sem.at[0]).wait()
 
@@ -297,11 +318,13 @@
         vm((k1 * OWN, 2 * LANES), BF16), vm((k1 * OWN, 2 * LANES), BF16), vm((rows, mixed), F32),
     ]
     dma = pltpu.SemaphoreType.DMA
-    sems = [dma((10,)), dma((nch,)), dma((nch,)), dma((2,)), dma((2,)), dma((2,)), dma((2,)), dma((nch,)), dma((nch,))]
+    sems = [
+        dma((10,)), dma((14,)), dma((nch, 2)), dma((2,)), dma((2,)), dma((2,)), dma((2,)), dma((14,)), dma((nch, 2)),
+    ]
     return pl.pallas_call(
         functools.partial(kernel, nctx, nch, 2),
         out_shape=jax.ShapeDtypeStruct((rows, mixed), BF16),
-        in_specs=[pl.BlockSpec(memory_space=pl.ANY)] * len(operands),
+        in_specs=[pl.BlockSpec(memory_space=pltpu.HBM)] * len(operands),
         out_specs=pl.BlockSpec(memory_space=pltpu.VMEM),
         scratch_shapes=scratch + sems,
         compiler_params=pltpu.CompilerParams(

time: 88.6 us -> 74.1 us (0.84)
  the two profiles are of different devices: /device:TPU:16 before, /device:TPU:6 now
where the time goes in v2:
time: 74.1 us; the launch traced here: 72.6 us
  Pallas kernels  60.8 us (82%)
  local copies, waits for them, and re-layouts  11.8 us (16%)
    pallas_call x1, Pallas kernels, shards(): pl.pallas_call(functools.partial(kernel, nctx, nch, 2), out_shape=jax.Sha...  60.8 us
    unnamed x21, local copies, waits for them, and re-layouts  11.8 us

profile of v2, /device:TPU:6, one launch (start us, length us, event | category | flops | bytes accessed | tf_op | source)
XLA Modules:
  0.0 72.6 jit_solution(12680417383611981462)
XLA Ops:
  0.0 0.0 copy-start
  0.0 2.8 %copy-done = bf16[4096,3,256]{2,0,1:T(8,128)(2,1)S(1)} copy-done((bf16[4096,3,256]{2,0,1:T(8,128)(2,1)S(1)}, bf16[4096,3,256]{2,0,1:T(8,128)(2,1)}, u32[]{:S(2)}) %copy-start) | copy-done | bytes 6291480
  2.8 0.0 copy-start.1
  2.8 1.6 %copy-done.1 = bf16[2048,512]{1,0:T(8,128)(2,1)S(1)} copy-done((bf16[2048,512]{1,0:T(8,128)(2,1)S(1)}, bf16[2048,512]{1,0:T(8,128)(2,1)}, u32[]{:S(2)}) %copy-start.1) | copy-done | bytes 2097176
  4.4 0.0 copy-start.2
  4.4 1.0 %copy-done.2 = bf16[4,256,256]{2,1,0:T(8,128)(2,1)S(1)} copy-done((bf16[4,256,256]{2,1,0:T(8,128)(2,1)S(1)}, bf16[4,256,256]{2,1,0:T(8,128)(2,1)}, u32[]{:S(2)}) %copy-start.2) | copy-done | bytes 524312
  5.4 0.0 copy-start.3
  5.4 0.9 %copy-done.3 = bf16[256,512]{1,0:T(8,128)(2,1)S(1)} copy-done((bf16[256,512]{1,0:T(8,128)(2,1)S(1)}, bf16[256,512]{1,0:T(8,128)(2,1)}, u32[]{:S(2)}) %copy-start.3) | copy-done | bytes 262168
  6.4 0.0 copy-start.4
  6.4 0.9 %copy-done.4 = f32[256,256]{1,0:T(8,128)S(1)} copy-done((f32[256,256]{1,0:T(8,128)S(1)}, f32[256,256]{1,0:T(8,128)}, u32[]{:S(2)}) %copy-start.4) | copy-done | bytes 262168
  7.3 0.0 copy-start.5
  7.3 0.8 %copy-done.5 = f32[2,64,128]{2,1,0:T(8,128)S(1)} copy-done((f32[2,64,128]{2,1,0:T(8,128)S(1)}, f32[2,64,128]{2,1,0:T(8,128)}, u32[]{:S(2)}) %copy-start.5) | copy-done | bytes 65560
  8.2 0.0 copy-start.6
  8.2 0.8 %copy-done.6 = bf16[2,128,64]{2,1,0:T(8,128)(2,1)S(1)} copy-done((bf16[2,128,64]{2,1,0:T(8,128)(2,1)S(1)}, bf16[2,128,64]{2,1,0:T(8,128)(2,1)}, u32[]{:S(2)}) %copy-start.6) | copy-done | bytes 32792
  9.0 0.0 copy-start.7
  9.0 0.8 %copy-done.7 = bf16[2,64,128]{2,1,0:T(8,128)(2,1)S(1)} copy-done((bf16[2,64,128]{2,1,0:T(8,128)(2,1)S(1)}, bf16[2,64,128]{2,1,0:T(8,128)(2,1)}, u32[]{:S(2)}) %copy-start.7) | copy-done | bytes 32792
  9.8 0.0 copy-start.8
  9.8 0.7 copy-done.8
  10.5 0.0 copy-start.9
  10.5 0.7 copy-done.9
  11.1 60.8 %shard_map.100 = bf16[256,512]{1,0:T(8,128)(2,1)S(1)} custom-call(bf16[256,512]{1,0:T(8,128)(2,1)S(1)} %copy-done.3, bf16[3,4096,256]{2,1,0:T(8,128)(2,1)S(1)} %bitcast.2, f32[3,3,256]{2,1,0:T(4,128)S(1)} %copy-done.8, f32[256,256]{1,0:T(8,128)S(1)} %copy-done.4, f32[1,256]{1,0:T(1,128)S(1)} %bitcast.3, bf16[2048,512]{1,0:T(8,128)(2,1)S(1)} %copy-done.1, ...), custom_call_target="tpu_custom_call" | custom-call | tf_op jit(solution)/shard_map/pallas_call | solution.py:324
  71.9 0.7 copy.12
Async XLA Ops:
  0.0 2.8 %copy-start = (bf16[4096,3,256]{2,0,1:T(8,128)(2,1)S(1)}, bf16[4096,3,256]{2,0,1:T(8,128)(2,1)}, u32[]{:S(2)}) copy-start(bf16[4096,3,256]{2,0,1:T(8,128)(2,1)} %param.11) | copy-start | bytes 18874372
  2.8 1.6 %copy-start.1 = (bf16[2048,512]{1,0:T(8,128)(2,1)S(1)}, bf16[2048,512]{1,0:T(8,128)(2,1)}, u32[]{:S(2)}) copy-start(bf16[2048,512]{1,0:T(8,128)(2,1)} %refs_5_.1) | copy-start | bytes 6291460
  4.4 1.0 %copy-start.2 = (bf16[4,256,256]{2,1,0:T(8,128)(2,1)S(1)}, bf16[4,256,256]{2,1,0:T(8,128)(2,1)}, u32[]{:S(2)}) copy-start(bf16[4,256,256]{2,1,0:T(8,128)(2,1)} %constant.10.clone.refs_8_) | copy-start | bytes 1572868
  5.4 0.9 %copy-start.3 = (bf16[256,512]{1,0:T(8,128)(2,1)S(1)}, bf16[256,512]{1,0:T(8,128)(2,1)}, u32[]{:S(2)}) copy-start(bf16[256,512]{1,0:T(8,128)(2,1)} %refs_0_.1) | copy-start | bytes 786436
  6.4 0.9 %copy-start.4 = (f32[256,256]{1,0:T(8,128)S(1)}, f32[256,256]{1,0:T(8,128)}, u32[]{:S(2)}) copy-start(f32[256,256]{1,0:T(8,128)} %refs_3_.1) | copy-start | bytes 786436
  7.3 0.8 %copy-start.5 = (f32[2,64,128]{2,1,0:T(8,128)S(1)}, f32[2,64,128]{2,1,0:T(8,128)}, u32[]{:S(2)}) copy-start(f32[2,64,128]{2,1,0:T(8,128)} %constant.11.clone.refs_9_) | copy-start | bytes 196612
  8.2 0.8 %copy-start.6 = (bf16[2,128,64]{2,1,0:T(8,128)(2,1)S(1)}, bf16[2,128,64]{2,1,0:T(8,128)(2,1)}, u32[]{:S(2)}) copy-start(bf16[2,128,64]{2,1,0:T(8,128)(2,1)} %constant.8.clone.refs_6_) | copy-start | bytes 98308
  9.0 0.8 %copy-start.7 = (bf16[2,64,128]{2,1,0:T(8,128)(2,1)S(1)}, bf16[2,64,128]{2,1,0:T(8,128)(2,1)}, u32[]{:S(2)}) copy-start(bf16[2,64,128]{2,1,0:T(8,128)(2,1)} %constant.9.clone.refs_7_) | copy-start | bytes 98308
  9.8 0.7 copy-start.8
  10.5 0.7 copy-start.9

commit v3 on v2

--- a/solution.py
+++ b/solution.py
@@ -45,6 +45,14 @@
     )
 
 
+def ctx_order(count):
+    size = (2, count // 4, 2) if count >= 4 else (1, 1, count)
+    nz = size[1]
+    far = sorted(range(nz), key=lambda z: -min(z, nz - z))
+    every = [(y, z, c) for z in far for y in reversed(range(size[0])) for c in reversed(range(size[2]))]
+    return size, [offset for offset in every if offset != (0, 0, 0)]
+
+
 def split(value):
     high = value.astype(BF16)
     return high, (value - high.astype(F32)).astype(BF16)
@@ -61,8 +69,8 @@
         out_ref,
         xg, w, taps, filt, skip, wo, first, last, mid, twist,
         proj, gate, gated, hsend, hrecv, gsend, grecv, csend, crecv, yg,
-        line, spec, hspec, dhi, dlo, acc,
-        local_sem, x_send, x_recv, halo_sem, h_sem, g_sem, c_sem, y_send, y_recv,
+        line, spec, hspec, dhi, dlo, acc, tail_out, tails, tail_x,
+        local_sem, x_send, x_recv, halo_sem, tail_sem, h_sem, g_sem, c_sem, y_send, y_recv,
     ) = refs
     ctx = lax.axis_index("ctx")
     ch = lax.axis_index("ch")
@@ -79,29 +87,42 @@
     own, plus, minus, two = at_ch(0, 0), at_ch(1, 0), at_ch(nx - 1, 0), at_ch(2, 0)
     own2, plus2, minus2, two2 = at_ch(0, 1), at_ch(1, 1), at_ch(nx - 1, 1), at_ch(2, 1)
 
-    def loads():
-        pairs = (
-            (x_hbm, xg.at[ch]), (filt_hbm, filt), (first_hbm, first), (mid_hbm, mid), (twist_hbm, twist),
-            (last_hbm, last), (taps_hbm, taps), (skip_hbm, skip), (w_hbm, w), (wo_hbm, wo),
-        )
-        return [pltpu.make_async_copy(s, d, local_sem.at[i]) for i, (s, d) in enumerate(pairs)]
-
-    local = loads()
+    size, offsets = ctx_order(nctx)
+
+    def ctx_peer(offset):
+        low = ctx % size[2]
+        z = (ctx // size[2]) % size[1]
+        y = ctx // (size[1] * size[2])
+        dy, dz, dc = offset
+        return (((y + dy) % size[0]) * size[1] + (z + dz) % size[1]) * size[2] + (low + dc) % size[2]
+
+    ctx_peers = [ctx_peer(offset) for offset in offsets]
+
+    pairs = (
+        (x_hbm, xg.at[own]), (filt_hbm, filt), (first_hbm, first), (mid_hbm, mid), (twist_hbm, twist),
+        (w_hbm, w), (last_hbm, last), (taps_hbm, taps), (skip_hbm, skip), (wo_hbm, wo),
+    )
+    local = [pltpu.make_async_copy(s, d, local_sem.at[i]) for i, (s, d) in enumerate(pairs)]
+    barrier = pltpu.get_barrier_semaphore()
+    for step in range(1, nch):
+        pl.semaphore_signal(barrier, inc=1, device_id={"ch": (ch + step) % nch}, device_id_type=MESH)
+    for to in ctx_peers:
+        pl.semaphore_signal(barrier, inc=1, device_id={"ctx": to}, device_id_type=MESH)
     for copy in local:
         copy.start()
 
-    barrier = pltpu.get_barrier_semaphore()
-
-    def greet_ctx(d, carry):
-        pl.semaphore_signal(barrier, inc=1, device_id={"ctx": (ctx + d) % nctx}, device_id_type=MESH)
-        return carry
-
-    def greet_ch(d, carry):
-        pl.semaphore_signal(barrier, inc=1, device_id={"ch": (ch + d) % nch}, device_id_type=MESH)
-        return carry
-
-    lax.fori_loop(1, nch, greet_ch, 0)
-    lax.fori_loop(1, nctx, greet_ctx, 0)
+    def to_parts(block):
+        turned = block.T.reshape(nctx, OWN, rows)
+        return jnp.concatenate([turned[:, :, :LANES], turned[:, :, LANES:]], axis=1)
+
+    for copy in local[:2]:
+        copy.wait()
+    hsend[...] = to_parts(filt[...])
+    tiles = feats // LANES
+    last_rows = xg[own, pl.ds(rows - 16, 16), :].astype(F32)
+    for r in range(2):
+        for part in range(tiles):
+            tail_out[pl.ds(r * tiles + part, 1), :] = last_rows[14 + r : 15 + r, part * LANES : (part + 1) * LANES]
     pl.semaphore_wait(barrier, nctx + nch - 2)
 
 
@@ -126,8 +147,8 @@
                 device_id={"ch": own2}, device_id_type=MESH,
             ).wait_recv()
 
-        def begin():
-            for h, to in ((0, own2), (0, plus), (1, minus), (1, own2), (1, plus), (0, minus)):
+        def begin(order):
+            for h, to in order:
                 push(own, h, to, source)
 
         def forward_first():
@@ -149,28 +170,25 @@
         return begin, forward_first, forward_second, pull, finish
 
     x_begin, x_first, x_second, x_pull, x_finish = gather(x_hbm, xg, x_send, x_recv)
-    x_begin()
+    x_begin(((0, own2), (0, plus), (1, minus), (1, own2), (1, plus), (0, minus)))
+    to_next = pltpu.make_async_remote_copy(
+        src_ref=tail_out, dst_ref=tails.at[own], send_sem=halo_sem.at[0], recv_sem=halo_sem.at[1],
+        device_id={"ctx": (ctx + 1) % nctx}, device_id_type=MESH,
+    )
+    to_next.start()
 
 
     def exchange(send, recv, sem):
-        def body(d, carry):
-            to = (ctx + d) % nctx
+        for to in ctx_peers:
             pltpu.make_async_remote_copy(
                 src_ref=send.at[to], dst_ref=recv.at[ctx], send_sem=sem.at[0], recv_sem=sem.at[1],
                 device_id={"ctx": to}, device_id_type=MESH,
             ).start()
-            return carry
-
-        lax.fori_loop(1, nctx, body, 0)
         recv[pl.ds(ctx, 1)] = send[pl.ds(ctx, 1)]
 
     def whole(send, sem):
         part = send.at[pl.ds(0, nctx - 1)]
         return pltpu.make_async_copy(part, part, sem)
-
-    def to_parts(block):
-        turned = block.T.reshape(nctx, OWN, rows)
-        return jnp.concatenate([turned[:, :, :LANES], turned[:, :, LANES:]], axis=1)
 
     def forward(result, exact):
         block = jnp.concatenate([line[pl.ds(c, k1, stride=OWN), :] for c in range(OWN)], axis=1)
@@ -204,12 +222,7 @@
         for c in range(OWN):
             line[pl.ds(c, k1, stride=OWN), :] = signal[:, c * LANES : (c + 1) * LANES]
 
-    for copy in local[1:6]:
-        copy.wait()
-    hsend[...] = to_parts(filt[...])
     exchange(hsend, hrecv, h_sem)
-    for copy in local[6:] + local[:1]:
-        copy.wait()
     top = 8
 
     def project(block, first_one=False):
@@ -220,8 +233,20 @@
             term = dot(part, w[s, at, :])
             proj[top:, cols] = term if first_one else proj[top:, cols] + term
 
+    to_next.wait_recv()
+    to_ch = [
+        pltpu.make_async_remote_copy(
+            src_ref=tails.at[own], dst_ref=tails.at[own], send_sem=tail_sem.at[0], recv_sem=tail_sem.at[1],
+            device_id={"ch": (ch + step) % nch}, device_id_type=MESH,
+        )
+        for step in range(1, nch)
+    ]
+    for copy in to_ch:
+        copy.start()
+    x_first()
+    for copy in local[2:]:
+        copy.wait()
     project(own, True)
-    x_first()
     for block in (own2, minus, plus):
         project(block)
 
@@ -229,19 +254,21 @@
     line[...] = hrecv[...].reshape(line.shape)
     forward(hspec, False)
     x_second()
+    others = tails.at[pl.ds(0, nch - 1)]
+    pltpu.make_async_copy(others, others, tail_sem.at[1]).wait()
+    tail_x[...] = jnp.zeros_like(tail_x)
+    for block in range(nch):
+        for r in range(2):
+            for part in range(tiles):
+                at = pl.ds(block * feats + part * LANES, LANES)
+                tail_x[pl.ds(top - 2 + r, 1), at] = tails[block, pl.ds(r * tiles + part, 1), :]
+    for s in range(3):
+        before = dot(tail_x[...].astype(BF16), w[s])
+        proj[:top, pl.ds(s * chans, chans)] = jnp.where(ctx == 0, 0.0, before)
     for block, waits in ((two, (0, 1)), (minus2, (1,)), (plus2, (0,)), (two2, (0, 1))):
         for h in waits:
             x_pull(block, h)
         project(block)
-    halo = pltpu.make_async_remote_copy(
-        src_ref=proj.at[pl.ds(rows, top)], dst_ref=proj.at[pl.ds(0, top)],
-        send_sem=halo_sem.at[0], recv_sem=halo_sem.at[1],
-        device_id={"ctx": (ctx + 1) % nctx}, device_id_type=MESH,
-    )
-    halo.start()
-    halo.wait()
-    proj[:top] = jnp.where(ctx == 0, 0.0, proj[:top])
-
     def stream(s):
         cols = pl.ds(s * chans, chans)
         return (
@@ -262,20 +289,19 @@
     csend[...] = line[...].reshape(csend.shape).astype(BF16)
     exchange(csend, crecv, c_sem)
     whole(csend, c_sem.at[1]).wait()
-    back = crecv[...].astype(F32)
-    for part in range(2):
+    y_begin, y_first, y_second, y_pull, y_finish = gather(yg.at[own], yg, y_send, y_recv)
+    for part, order in ((0, (own2, plus, minus)), (1, (own2, minus, plus))):
         at = pl.ds(part * LANES, LANES)
-        conv = back[:, part * OWN : (part + 1) * OWN, :].reshape(chans, LANES).T
+        back = crecv[:, part * OWN : (part + 1) * OWN, :].astype(F32)
+        conv = back.reshape(chans, LANES).T
         mixed = gate[at, :] * (conv + skip[...] * gated[at, :])
         yg[own, at, :] = mixed.astype(BF16)
-
-    y_begin, y_first, y_second, y_pull, y_finish = gather(yg.at[own], yg, y_send, y_recv)
+        y_begin([(part, to) for to in order])
 
     def mix(block):
         at = pl.ds(pl.multiple_of(block * chans, chans), chans)
         return dot(yg[block], wo[at, :])
 
-    y_begin()
     acc[...] = mix(own)
     y_first()
     for block in (own2, minus, plus):
@@ -289,6 +315,8 @@
 
     x_finish()
     y_finish()
+    to_next.wait_send()
+    pltpu.make_async_copy(others, others, tail_sem.at[0]).wait()
     whole(hsend, h_sem.at[0]).wait()
     whole(gsend, g_sem.at[0]).wait()
     whole(csend, c_sem.at[0]).wait()
@@ -316,10 +344,12 @@
         vm((nch, rows, chans), BF16),
         vm((k1 * OWN, LANES), F32), vm((k1 * OWN, 2 * LANES), F32), vm((k1 * OWN, 2 * LANES), F32),
         vm((k1 * OWN, 2 * LANES), BF16), vm((k1 * OWN, 2 * LANES), BF16), vm((rows, mixed), F32),
+        vm((2 * feats // LANES, LANES), F32), vm((nch, 2 * feats // LANES, LANES), F32), vm((8, width), F32),
     ]
     dma = pltpu.SemaphoreType.DMA
     sems = [
-        dma((10,)), dma((14,)), dma((nch, 2)), dma((2,)), dma((2,)), dma((2,)), dma((2,)), dma((14,)), dma((nch, 2)),
+        dma((10,)), dma((14,)), dma((nch, 2)), dma((2,)), dma((2,)), dma((2,)), dma((2,)), dma((2,)),
+        dma((14,)), dma((nch, 2)),
     ]
     return pl.pallas_call(
         functools.partial(kernel, nctx, nch, 2),
@@ -328,7 +358,7 @@
         out_specs=pl.BlockSpec(memory_space=pltpu.VMEM),
         scratch_shapes=scratch + sems,
         compiler_params=pltpu.CompilerParams(
-            collective_id=0, has_side_effects=True, vmem_limit_bytes=40 * 1024 * 1024
+            collective_id=0, has_side_effects=True, vmem_limit_bytes=63 * 1024 * 1024
         ),
     )(*operands)
 

time: 74.1 us -> 59 us (0.80)
  local copies, waits for them, and re-layouts: 11.8 us -> 1.67 us
  Pallas kernels: 60.8 us -> 56.4 us
    unnamed x21 -> x1, local copies, waits for them, and re-layouts: 11.8 us -> 1.67 us
    pallas_call x1, Pallas kernels: 60.8 us -> 56.4 us  [shards(): pl.pallas_call(functools.partial(kernel, nctx, nch, 2), out_shape=jax.Sha...]
where the time goes in v3:
time: 59 us; the launch traced here: 58.1 us
  Pallas kernels  56.4 us (96%)
  local copies, waits for them, and re-layouts  1.67 us (3%)
    pallas_call x1, Pallas kernels, shards(): pl.pallas_call(functools.partial(kernel, nctx, nch, 2), out_shape=jax.Sha...  56.4 us
    unnamed x1, local copies, waits for them, and re-layouts  1.67 us

profile of v3, /device:TPU:6, one launch (start us, length us, event | category | flops | bytes accessed | tf_op | source)
XLA Modules:
  0.0 58.1 jit_solution(8727975476101892877)
XLA Ops:
  0.0 56.4 %shard_map.100 = bf16[256,512]{1,0:T(8,128)(2,1)} custom-call(bf16[256,512]{1,0:T(8,128)(2,1)} %refs_0_.1, bf16[3,4096,256]{2,1,0:T(8,128)(2,1)} %bitcast.2, f32[3,3,256]{2,1,0:T(4,128)} %refs_2_.1, f32[256,256]{1,0:T(8,128)} %refs_3_.1, f32[1,256]{1,0:T(1,128)} %bitcast.3, bf16[2048,512]{1,0:T(8,128)(2,1)} %refs_5_.1, ...), custom_call_target="tpu_custom_call" | custom-call | tf_op jit(solution)/shard_map/pallas_call | solution.py:354
  56.5 1.7 %copy.12 = bf16[256,512]{1,0:T(8,128)(2,1)} copy(bf16[256,512]{1,0:T(8,128)(2,1)} %shard_map.100) | data formatting | bytes 524288

commit v4 on v3

--- a/solution.py
+++ b/solution.py
@@ -70,7 +70,7 @@
         xg, w, taps, filt, skip, wo, first, last, mid, twist,
         proj, gate, gated, hsend, hrecv, gsend, grecv, csend, crecv, yg,
         line, spec, hspec, dhi, dlo, acc, tail_out, tails, tail_x,
-        local_sem, x_send, x_recv, halo_sem, tail_sem, h_sem, g_sem, c_sem, y_send, y_recv,
+        heard, local_sem, x_send, x_recv, halo_sem, tail_sem, h_sem, g_sem, c_sem, y_send, y_recv,
     ) = refs
     ctx = lax.axis_index("ctx")
     ch = lax.axis_index("ch")
@@ -103,11 +103,29 @@
         (w_hbm, w), (last_hbm, last), (taps_hbm, taps), (skip_hbm, skip), (wo_hbm, wo),
     )
     local = [pltpu.make_async_copy(s, d, local_sem.at[i]) for i, (s, d) in enumerate(pairs)]
+    ways = [(0, 0, 1)] if size[2] > 1 else []
+    z_ways = [(0, 1, 0), (0, size[1] - 1, 0)] if size[1] > 1 else []
+    y_ways = [(1, 0, 0)] if size[0] > 1 else []
     barrier = pltpu.get_barrier_semaphore()
-    for step in range(1, nch):
-        pl.semaphore_signal(barrier, inc=1, device_id={"ch": (ch + step) % nch}, device_id_type=MESH)
-    for to in ctx_peers:
-        pl.semaphore_signal(barrier, inc=1, device_id={"ctx": to}, device_id_type=MESH)
+
+    def greet(sem, chs, offs):
+        for to in chs:
+            pl.semaphore_signal(sem, inc=1, device_id={"ch": to}, device_id_type=MESH)
+        for offset in offs:
+            pl.semaphore_signal(sem, inc=1, device_id={"ctx": ctx_peer(offset)}, device_id_type=MESH)
+
+    near = (plus, minus, own2)
+    rounds = [(near, ways), ((own2,), z_ways)] + [((), z_ways)] * 3
+
+    def tell(i):
+        greet(heard.at[i], *rounds[i])
+
+    def hear(i):
+        count = len(rounds[i][0]) + len(rounds[i][1])
+        if count:
+            pl.semaphore_wait(heard.at[i], count)
+
+    greet(barrier, near, ways + y_ways + z_ways)
     for copy in local:
         copy.start()
 
@@ -123,7 +141,7 @@
     for r in range(2):
         for part in range(tiles):
             tail_out[pl.ds(r * tiles + part, 1), :] = last_rows[14 + r : 15 + r, part * LANES : (part + 1) * LANES]
-    pl.semaphore_wait(barrier, nctx + nch - 2)
+    pl.semaphore_wait(barrier, len(near) + len(ways + y_ways + z_ways))
 
 
     def gather(source, slots, send, recv):
@@ -151,11 +169,15 @@
             for h, to in order:
                 push(own, h, to, source)
 
-        def forward_first():
+        def forward_own2():
             pull(own2, 0), push(own2, 0, plus)
             pull(own2, 1), push(own2, 1, minus)
+
+        def forward_near():
             pull(minus, 0), push(minus, 0, plus)
             pull(plus, 1), push(plus, 1, minus)
+
+        def cross():
             pull(minus, 1), push(minus, 1, own2)
             pull(plus, 0), push(plus, 0, own2)
 
@@ -167,7 +189,7 @@
             for copy in started:
                 copy.wait_send()
 
-        return begin, forward_first, forward_second, pull, finish
+        return begin, (forward_own2, forward_near, cross), forward_second, pull, finish
 
     x_begin, x_first, x_second, x_pull, x_finish = gather(x_hbm, xg, x_send, x_recv)
     x_begin(((0, own2), (0, plus), (1, minus), (1, own2), (1, plus), (0, minus)))
@@ -175,6 +197,11 @@
         src_ref=tail_out, dst_ref=tails.at[own], send_sem=halo_sem.at[0], recv_sem=halo_sem.at[1],
         device_id={"ctx": (ctx + 1) % nctx}, device_id_type=MESH,
     )
+    tell(0)
+    hear(0)
+    tell(1)
+    hear(1)
+    tell(2)
     to_next.start()
 
 
@@ -222,7 +249,6 @@
         for c in range(OWN):
             line[pl.ds(c, k1, stride=OWN), :] = signal[:, c * LANES : (c + 1) * LANES]
 
-    exchange(hsend, hrecv, h_sem)
     top = 8
 
     def project(block, first_one=False):
@@ -233,6 +259,12 @@
             term = dot(part, w[s, at, :])
             proj[top:, cols] = term if first_one else proj[top:, cols] + term
 
+    x_first[0]()
+    hear(2)
+    tell(3)
+    x_first[1]()
+    hear(3)
+    tell(4)
     to_next.wait_recv()
     to_ch = [
         pltpu.make_async_remote_copy(
@@ -243,17 +275,16 @@
     ]
     for copy in to_ch:
         copy.start()
-    x_first()
+    x_first[2]()
+    hear(4)
     for copy in local[2:]:
         copy.wait()
     project(own, True)
     for block in (own2, minus, plus):
         project(block)
 
-    whole(hsend, h_sem.at[1]).wait()
-    line[...] = hrecv[...].reshape(line.shape)
-    forward(hspec, False)
     x_second()
+    exchange(hsend, hrecv, h_sem)
     others = tails.at[pl.ds(0, nch - 1)]
     pltpu.make_async_copy(others, others, tail_sem.at[1]).wait()
     tail_x[...] = jnp.zeros_like(tail_x)
@@ -281,6 +312,9 @@
     gsend[...] = to_parts(gated[...]).astype(BF16)
     exchange(gsend, grecv, g_sem)
     gate[...] = stream(1)
+    whole(hsend, h_sem.at[1]).wait()
+    line[...] = hrecv[...].reshape(line.shape)
+    forward(hspec, False)
     whole(gsend, g_sem.at[1]).wait()
 
     line[...] = grecv[...].astype(F32).reshape(line.shape)
@@ -303,7 +337,8 @@
         return dot(yg[block], wo[at, :])
 
     acc[...] = mix(own)
-    y_first()
+    for forward_part in y_first:
+        forward_part()
     for block in (own2, minus, plus):
         acc[...] += mix(block)
     y_second()
@@ -348,19 +383,19 @@
     ]
     dma = pltpu.SemaphoreType.DMA
     sems = [
-        dma((10,)), dma((14,)), dma((nch, 2)), dma((2,)), dma((2,)), dma((2,)), dma((2,)), dma((2,)),
+        pltpu.SemaphoreType.REGULAR((5,)), dma((10,)), dma((14,)), dma((nch, 2)), dma((2,)), dma((2,)), dma((2,)), dma((2,)), dma((2,)),
         dma((14,)), dma((nch, 2)),
     ]
     return pl.pallas_call(
         functools.partial(kernel, nctx, nch, 2),
-        out_shape=jax.ShapeDtypeStruct((rows, mixed), BF16),
+        out_shape=pltpu.VMEM((rows, mixed), BF16),
         in_specs=[pl.BlockSpec(memory_space=pltpu.HBM)] * len(operands),
         out_specs=pl.BlockSpec(memory_space=pltpu.VMEM),
         scratch_shapes=scratch + sems,
         compiler_params=pltpu.CompilerParams(
-            collective_id=0, has_side_effects=True, vmem_limit_bytes=63 * 1024 * 1024
+            collective_id=0, has_side_effects=True, vmem_limit_bytes=60 * 1024 * 1024
         ),
-    )(*operands)
+    )(*[pltpu.with_memory_space_constraint(o, pltpu.HBM) for o in operands])
 
 
 def solution(mesh):

time: 59 us -> 55.1 us (0.934); the launches traced: 58.1 us -> 55 us
  Pallas kernels: 56.4 us -> 54.3 us
  local copies, waits for them, and re-layouts: 1.67 us -> 0.71 us
    pallas_call x1, Pallas kernels: 56.4 us -> 54.3 us  [shards(): pl.pallas_call(functools.partial(kernel, nctx, nch, 2), out_shape=pltpu.V...]
    unnamed x1, local copies, waits for them, and re-layouts: 1.67 us -> 0.71 us
where the time goes in v4:
time: 55.1 us; the launch traced here: 55 us
  Pallas kernels  54.3 us (99%)
  local copies, waits for them, and re-layouts  0.71 us (1%)
    pallas_call x1, Pallas kernels, shards(): pl.pallas_call(functools.partial(kernel, nctx, nch, 2), out_shape=pltpu.V...  54.3 us

profile of v4, /device:TPU:6, one launch (start us, length us, event | category | flops | bytes accessed | tf_op | source)
XLA Modules:
  0.0 55.0 jit_solution(17301262923632655487)
XLA Ops:
  0.0 54.3 %shard_map.100 = bf16[256,512]{1,0:T(8,128)(2,1)S(1)} custom-call(bf16[256,512]{1,0:T(8,128)(2,1)} %refs_0_.1, bf16[3,4096,256]{2,1,0:T(8,128)(2,1)} %bitcast.2, f32[3,3,256]{2,1,0:T(4,128)} %refs_2_.1, f32[256,256]{1,0:T(8,128)} %refs_3_.1, f32[1,256]{1,0:T(1,128)} %bitcast.3, bf16[2048,512]{1,0:T(8,128)(2,1)} %refs_5_.1, ...), custom_call_target="tpu_custom_call" | custom-call | tf_op jit(solution)/shard_map/pallas_call | solution.py:389
  54.3 0.7 %copy.12 = bf16[256,512]{1,0:T(8,128)(2,1)} copy(bf16[256,512]{1,0:T(8,128)(2,1)S(1)} %shard_map.100) | data formatting | bytes 524288

commit v5 on v4

--- a/solution.py
+++ b/solution.py
@@ -133,6 +133,53 @@
         turned = block.T.reshape(nctx, OWN, rows)
         return jnp.concatenate([turned[:, :, :LANES], turned[:, :, LANES:]], axis=1)
 
+    pl.semaphore_wait(barrier, len(near) + len(ways + y_ways + z_ways))
+
+
+    core = ctx % size[2]
+
+    def on(only, act):
+        if only is None:
+            act()
+        else:
+            pl.when(core == only)(act)
+
+    def gather(source, slots, send, recv):
+        started = []
+
+        def piece(block, h):
+            return slots.at[block, pl.ds(h * half, half)]
+
+        def push(block, h, to, src=None, only=None):
+            copy = pltpu.make_async_remote_copy(
+                src_ref=piece(block, h) if src is None else src.at[pl.ds(h * half, half)],
+                dst_ref=piece(block, h), send_sem=send.at[len(started)], recv_sem=recv.at[block, h],
+                device_id={"ch": to}, device_id_type=MESH,
+            )
+            on(only, copy.start)
+            started.append((only, copy))
+
+        def pull(block, h, only=None):
+            copy = pltpu.make_async_remote_copy(
+                src_ref=piece(block, h), dst_ref=piece(block, h), send_sem=send.at[0], recv_sem=recv.at[block, h],
+                device_id={"ch": own2}, device_id_type=MESH,
+            )
+            on(only, copy.wait_recv)
+
+        def finish():
+            for only, copy in started:
+                on(only, copy.wait_send)
+
+        return push, pull, finish
+
+    x_push, x_pull, x_finish = gather(x_hbm, xg, x_send, x_recv)
+    for h, to in ((0, own2), (0, plus), (1, minus), (1, own2), (1, plus), (0, minus)):
+        x_push(own, h, to, x_hbm)
+    to_next = pltpu.make_async_remote_copy(
+        src_ref=tail_out, dst_ref=tails.at[own], send_sem=halo_sem.at[0], recv_sem=halo_sem.at[1],
+        device_id={"ctx": (ctx + 1) % nctx}, device_id_type=MESH,
+    )
+    tell(0)
     for copy in local[:2]:
         copy.wait()
     hsend[...] = to_parts(filt[...])
@@ -141,63 +188,6 @@
     for r in range(2):
         for part in range(tiles):
             tail_out[pl.ds(r * tiles + part, 1), :] = last_rows[14 + r : 15 + r, part * LANES : (part + 1) * LANES]
-    pl.semaphore_wait(barrier, len(near) + len(ways + y_ways + z_ways))
-
-
-    def gather(source, slots, send, recv):
-        started = []
-
-        def piece(block, h):
-            return slots.at[block, pl.ds(h * half, half)]
-
-        def push(block, h, to, src=None):
-            copy = pltpu.make_async_remote_copy(
-                src_ref=piece(block, h) if src is None else src.at[pl.ds(h * half, half)],
-                dst_ref=piece(block, h), send_sem=send.at[len(started)], recv_sem=recv.at[block, h],
-                device_id={"ch": to}, device_id_type=MESH,
-            )
-            copy.start()
-            started.append(copy)
-
-        def pull(block, h):
-            pltpu.make_async_remote_copy(
-                src_ref=piece(block, h), dst_ref=piece(block, h), send_sem=send.at[0], recv_sem=recv.at[block, h],
-                device_id={"ch": own2}, device_id_type=MESH,
-            ).wait_recv()
-
-        def begin(order):
-            for h, to in order:
-                push(own, h, to, source)
-
-        def forward_own2():
-            pull(own2, 0), push(own2, 0, plus)
-            pull(own2, 1), push(own2, 1, minus)
-
-        def forward_near():
-            pull(minus, 0), push(minus, 0, plus)
-            pull(plus, 1), push(plus, 1, minus)
-
-        def cross():
-            pull(minus, 1), push(minus, 1, own2)
-            pull(plus, 0), push(plus, 0, own2)
-
-        def forward_second():
-            pull(minus2, 0), push(minus2, 0, plus)
-            pull(plus2, 1), push(plus2, 1, minus)
-
-        def finish():
-            for copy in started:
-                copy.wait_send()
-
-        return begin, (forward_own2, forward_near, cross), forward_second, pull, finish
-
-    x_begin, x_first, x_second, x_pull, x_finish = gather(x_hbm, xg, x_send, x_recv)
-    x_begin(((0, own2), (0, plus), (1, minus), (1, own2), (1, plus), (0, minus)))
-    to_next = pltpu.make_async_remote_copy(
-        src_ref=tail_out, dst_ref=tails.at[own], send_sem=halo_sem.at[0], recv_sem=halo_sem.at[1],
-        device_id={"ctx": (ctx + 1) % nctx}, device_id_type=MESH,
-    )
-    tell(0)
     hear(0)
     tell(1)
     hear(1)
@@ -259,10 +249,12 @@
             term = dot(part, w[s, at, :])
             proj[top:, cols] = term if first_one else proj[top:, cols] + term
 
-    x_first[0]()
+    x_pull(minus, 0), x_push(minus, 0, plus)
+    x_pull(plus, 1), x_push(plus, 1, minus)
     hear(2)
     tell(3)
-    x_first[1]()
+    x_pull(own2, 0), x_push(own2, 0, plus), x_push(own2, 0, minus, only=0)
+    x_pull(own2, 1), x_push(own2, 1, minus), x_push(own2, 1, plus, only=0)
     hear(3)
     tell(4)
     to_next.wait_recv()
@@ -275,15 +267,18 @@
     ]
     for copy in to_ch:
         copy.start()
-    x_first[2]()
+    x_pull(minus, 1, only=1), x_push(minus, 1, own2, only=1)
+    x_pull(plus, 0, only=1), x_push(plus, 0, own2, only=1)
+    for h in range(2):
+        x_pull(two, h), x_push(two, h, own2, only=0)
     hear(4)
     for copy in local[2:]:
         copy.wait()
     project(own, True)
-    for block in (own2, minus, plus):
-        project(block)
-
-    x_second()
+    project(own2)
+
+    x_pull(minus2, 0), x_push(minus2, 0, plus, only=1)
+    x_pull(plus2, 1), x_push(plus2, 1, minus, only=1)
     exchange(hsend, hrecv, h_sem)
     others = tails.at[pl.ds(0, nch - 1)]
     pltpu.make_async_copy(others, others, tail_sem.at[1]).wait()
@@ -296,7 +291,10 @@
     for s in range(3):
         before = dot(tail_x[...].astype(BF16), w[s])
         proj[:top, pl.ds(s * chans, chans)] = jnp.where(ctx == 0, 0.0, before)
-    for block, waits in ((two, (0, 1)), (minus2, (1,)), (plus2, (0,)), (two2, (0, 1))):
+    x_pull(minus, 1, only=0), x_pull(plus, 0, only=0)
+    for block in (two, minus, plus):
+        project(block)
+    for block, waits in ((minus2, (1,)), (plus2, (0,)), (two2, (0, 1))):
         for h in waits:
             x_pull(block, h)
         project(block)
@@ -323,25 +321,33 @@
     csend[...] = line[...].reshape(csend.shape).astype(BF16)
     exchange(csend, crecv, c_sem)
     whole(csend, c_sem.at[1]).wait()
-    y_begin, y_first, y_second, y_pull, y_finish = gather(yg.at[own], yg, y_send, y_recv)
+    y_push, y_pull, y_finish = gather(yg.at[own], yg, y_send, y_recv)
     for part, order in ((0, (own2, plus, minus)), (1, (own2, minus, plus))):
         at = pl.ds(part * LANES, LANES)
         back = crecv[:, part * OWN : (part + 1) * OWN, :].astype(F32)
         conv = back.reshape(chans, LANES).T
         mixed = gate[at, :] * (conv + skip[...] * gated[at, :])
         yg[own, at, :] = mixed.astype(BF16)
-        y_begin([(part, to) for to in order])
+        for to in order:
+            y_push(own, part, to)
+    for h in range(2):
+        y_push(own, h, two2, only=0)
 
     def mix(block):
         at = pl.ds(pl.multiple_of(block * chans, chans), chans)
         return dot(yg[block], wo[at, :])
 
     acc[...] = mix(own)
-    for forward_part in y_first:
-        forward_part()
+    y_pull(own2, 0), y_push(own2, 0, plus)
+    y_pull(own2, 1), y_push(own2, 1, minus)
+    y_pull(minus, 0), y_push(minus, 0, plus)
+    y_pull(plus, 1), y_push(plus, 1, minus)
+    y_pull(minus, 1), y_push(minus, 1, own2)
+    y_pull(plus, 0), y_push(plus, 0, own2)
     for block in (own2, minus, plus):
         acc[...] += mix(block)
-    y_second()
+    y_pull(minus2, 0), y_push(minus2, 0, plus, only=1)
+    y_pull(plus2, 1), y_push(plus2, 1, minus, only=1)
     for block, waits in ((two, (0, 1)), (minus2, (1,)), (plus2, (0,)), (two2, (0, 1))):
         for h in waits:
             y_pull(block, h)
@@ -383,8 +389,8 @@
     ]
     dma = pltpu.SemaphoreType.DMA
     sems = [
-        pltpu.SemaphoreType.REGULAR((5,)), dma((10,)), dma((14,)), dma((nch, 2)), dma((2,)), dma((2,)), dma((2,)), dma((2,)), dma((2,)),
-        dma((14,)), dma((nch, 2)),
+        pltpu.SemaphoreType.REGULAR((5,)), dma((10,)), dma((18,)), dma((nch, 2)), dma((2,)), dma((2,)), dma((2,)), dma((2,)), dma((2,)),
+        dma((16,)), dma((nch, 2)),
     ]
     return pl.pallas_call(
         functools.partial(kernel, nctx, nch, 2),

time: 55.1 us -> 54 us (0.980)
  Pallas kernels: 54.3 us -> 53.3 us
    pallas_call x1, Pallas kernels: 54.3 us -> 53.3 us  [shards(): pl.pallas_call(functools.partial(kernel, nctx, nch, 2), out_shape=pltpu.V...]
where the time goes in v5:
time: 54 us
  Pallas kernels  53.3 us (99%)
  local copies, waits for them, and re-layouts  0.71 us (1%)
    pallas_call x1, Pallas kernels, shards(): pl.pallas_call(functools.partial(kernel, nctx, nch, 2), out_shape=pltpu.V...  53.3 us

profile of v5, /device:TPU:6, one launch (start us, length us, event | category | flops | bytes accessed | tf_op | source)
XLA Modules:
  0.0 54.0 jit_solution(15095041551491991682)
XLA Ops:
  0.0 53.3 %shard_map.100 = bf16[256,512]{1,0:T(8,128)(2,1)S(1)} custom-call(bf16[256,512]{1,0:T(8,128)(2,1)} %refs_0_.1, bf16[3,4096,256]{2,1,0:T(8,128)(2,1)} %bitcast.2, f32[3,3,256]{2,1,0:T(4,128)} %refs_2_.1, f32[256,256]{1,0:T(8,128)} %refs_3_.1, f32[1,256]{1,0:T(1,128)} %bitcast.3, bf16[2048,512]{1,0:T(8,128)(2,1)} %refs_5_.1, ...), custom_call_target="tpu_custom_call" | custom-call | tf_op jit(solution)/shard_map/pallas_call | solution.py:395
  53.3 0.7 %copy.12 = bf16[256,512]{1,0:T(8,128)(2,1)} copy(bf16[256,512]{1,0:T(8,128)(2,1)S(1)} %shard_map.100) | data formatting | bytes 524288

commit v6 on v5

--- a/solution.py
+++ b/solution.py
@@ -125,8 +125,9 @@
         if count:
             pl.semaphore_wait(heard.at[i], count)
 
+    local[0].start()
     greet(barrier, near, ways + y_ways + z_ways)
-    for copy in local:
+    for copy in local[1:]:
         copy.start()
 
     def to_parts(block):
@@ -172,16 +173,16 @@
 
         return push, pull, finish
 
+    local[0].wait()
     x_push, x_pull, x_finish = gather(x_hbm, xg, x_send, x_recv)
     for h, to in ((0, own2), (0, plus), (1, minus), (1, own2), (1, plus), (0, minus)):
-        x_push(own, h, to, x_hbm)
+        x_push(own, h, to)
     to_next = pltpu.make_async_remote_copy(
         src_ref=tail_out, dst_ref=tails.at[own], send_sem=halo_sem.at[0], recv_sem=halo_sem.at[1],
         device_id={"ctx": (ctx + 1) % nctx}, device_id_type=MESH,
     )
     tell(0)
-    for copy in local[:2]:
-        copy.wait()
+    local[1].wait()
     hsend[...] = to_parts(filt[...])
     tiles = feats // LANES
     last_rows = xg[own, pl.ds(rows - 16, 16), :].astype(F32)

time: 54 us -> 53.7 us (level)
  no operation moved by 1% of the time
where the time goes in v6:
time: 53.7 us; the launch traced here: 53.6 us
  Pallas kernels  52.9 us (99%)
  local copies, waits for them, and re-layouts  0.71 us (1%)
    pallas_call x1, Pallas kernels, shards(): pl.pallas_call(functools.partial(kernel, nctx, nch, 2), out_shape=pltpu.V...  52.9 us

profile of v6, /device:TPU:6, one launch (start us, length us, event | category | flops | bytes accessed | tf_op | source)
XLA Modules:
  0.0 53.6 jit_solution(1861096929543967919)
XLA Ops:
  0.0 52.9 %shard_map.100 = bf16[256,512]{1,0:T(8,128)(2,1)S(1)} custom-call(bf16[256,512]{1,0:T(8,128)(2,1)} %refs_0_.1, bf16[3,4096,256]{2,1,0:T(8,128)(2,1)} %bitcast.2, f32[3,3,256]{2,1,0:T(4,128)} %refs_2_.1, f32[256,256]{1,0:T(8,128)} %refs_3_.1, f32[1,256]{1,0:T(1,128)} %bitcast.3, bf16[2048,512]{1,0:T(8,128)(2,1)} %refs_5_.1, ...), custom_call_target="tpu_custom_call" | custom-call | tf_op jit(solution)/shard_map/pallas_call | solution.py:396
  52.9 0.7 %copy.12 = bf16[256,512]{1,0:T(8,128)(2,1)} copy(bf16[256,512]{1,0:T(8,128)(2,1)S(1)} %shard_map.100) | data formatting | bytes 524288

commit v7 on v6

--- a/solution.py
+++ b/solution.py
@@ -323,10 +323,10 @@
     exchange(csend, crecv, c_sem)
     whole(csend, c_sem.at[1]).wait()
     y_push, y_pull, y_finish = gather(yg.at[own], yg, y_send, y_recv)
+    back = crecv[...].astype(F32)
     for part, order in ((0, (own2, plus, minus)), (1, (own2, minus, plus))):
         at = pl.ds(part * LANES, LANES)
-        back = crecv[:, part * OWN : (part + 1) * OWN, :].astype(F32)
-        conv = back.reshape(chans, LANES).T
+        conv = back[:, part * OWN : (part + 1) * OWN, :].reshape(chans, LANES).T
         mixed = gate[at, :] * (conv + skip[...] * gated[at, :])
         yg[own, at, :] = mixed.astype(BF16)
         for to in order:

time: 53.7 us -> 53.7 us (level)
  no operation moved by 1% of the time
where the time goes in v7:
time: 53.7 us; the launch traced here: 53.6 us
  Pallas kernels  52.9 us (99%)
  local copies, waits for them, and re-layouts  0.71 us (1%)
    pallas_call x1, Pallas kernels, shards(): pl.pallas_call(functools.partial(kernel, nctx, nch, 2), out_shape=pltpu.V...  52.9 us

profile of v7, /device:TPU:6, one launch (start us, length us, event | category | flops | bytes accessed | tf_op | source)
XLA Modules:
  0.0 53.6 jit_solution(14764098114845074615)
XLA Ops:
  0.0 52.9 %shard_map.100 = bf16[256,512]{1,0:T(8,128)(2,1)S(1)} custom-call(bf16[256,512]{1,0:T(8,128)(2,1)} %refs_0_.1, bf16[3,4096,256]{2,1,0:T(8,128)(2,1)} %bitcast.2, f32[3,3,256]{2,1,0:T(4,128)} %refs_2_.1, f32[256,256]{1,0:T(8,128)} %refs_3_.1, f32[1,256]{1,0:T(1,128)} %bitcast.3, bf16[2048,512]{1,0:T(8,128)(2,1)} %refs_5_.1, ...), custom_call_target="tpu_custom_call" | custom-call | tf_op jit(solution)/shard_map/pallas_call | solution.py:396
  52.9 0.7 %copy.12 = bf16[256,512]{1,0:T(8,128)(2,1)} copy(bf16[256,512]{1,0:T(8,128)(2,1)S(1)} %shard_map.100) | data formatting | bytes 524288

commit v8 on v7

--- a/solution.py
+++ b/solution.py
@@ -38,9 +38,9 @@
     second = np.block([[cosine, -sine], [sine, cosine]])
     back = np.block([[cosine, sine], [-sine, cosine]])
     return (
-        halves(first),
-        halves(first.T / length),
-        np.concatenate([halves(second), halves(back)]),
+        np.concatenate(list(halves(first)), 1),
+        np.concatenate([halves(first.T / length)[i] for i in (0, 1, 0)], 1),
+        np.stack([np.concatenate([halves(t)[i] for i in (0, 0, 1)]) for t in (second, back)]),
         twist,
     )
 
@@ -69,14 +69,14 @@
         out_ref,
         xg, w, taps, filt, skip, wo, first, last, mid, twist,
         proj, gate, gated, hsend, hrecv, gsend, grecv, csend, crecv, yg,
-        line, spec, hspec, dhi, dlo, acc, tail_out, tails, tail_x,
+        line, spec, hspec, parts3, acc, tail_out, tails, tail_x,
         heard, local_sem, x_send, x_recv, halo_sem, tail_sem, h_sem, g_sem, c_sem, y_send, y_recv,
     ) = refs
     ctx = lax.axis_index("ctx")
     ch = lax.axis_index("ch")
     rows, feats = x_hbm.shape
     chans = filt_hbm.shape[1]
-    k1 = first_hbm.shape[2]
+    k1 = first_hbm.shape[0] // 2
 
     nx = nch // ny
     half = rows // 2
@@ -208,26 +208,32 @@
         part = send.at[pl.ds(0, nctx - 1)]
         return pltpu.make_async_copy(part, part, sem)
 
+    def lay(at, col, value):
+        high, low = split(value)
+        for i, half_value in enumerate((high, low, high)):
+            parts3[at, col + 2 * LANES * i : col + 2 * LANES * i + LANES] = half_value
+
     def forward(result, exact):
         block = jnp.concatenate([line[pl.ds(c, k1, stride=OWN), :] for c in range(OWN)], axis=1)
         high, low = split(block)
-        turned = dot(first[0], high) + dot(first[1], high)
+        turned = dot(first[...], jnp.concatenate([high, high], axis=0))
         if not exact:
-            turned = turned + dot(first[0], low)
+            turned = turned + dot(first[...], jnp.concatenate([low, jnp.zeros_like(low)], axis=0))
         for c in range(OWN):
             real = turned[:k1, c * LANES : (c + 1) * LANES]
             imag = turned[k1:, c * LANES : (c + 1) * LANES]
             at = pl.ds(c * k1, k1)
-            dhi[at, :LANES], dlo[at, :LANES] = split(real * twist[0] - imag * twist[1])
-            dhi[at, LANES:], dlo[at, LANES:] = split(real * twist[1] + imag * twist[0])
-        result[...] = dot(dhi[...], mid[0]) + dot(dhi[...], mid[1]) + dot(dlo[...], mid[0])
+            lay(at, 0, real * twist[0] - imag * twist[1])
+            lay(at, LANES, real * twist[1] + imag * twist[0])
+        result[...] = dot(parts3[...], mid[0])
 
     def backward():
         xr, xi = spec[:, :LANES], spec[:, LANES:]
         hr, hi = hspec[:, :LANES], hspec[:, LANES:]
-        dhi[:, :LANES], dlo[:, :LANES] = split(xr * hr - xi * hi)
-        dhi[:, LANES:], dlo[:, LANES:] = split(xr * hi + xi * hr)
-        spec[...] = dot(dhi[...], mid[2]) + dot(dhi[...], mid[3]) + dot(dlo[...], mid[2])
+        every = slice(None)
+        lay(every, 0, xr * hr - xi * hi)
+        lay(every, LANES, xr * hi + xi * hr)
+        spec[...] = dot(parts3[...], mid[1])
         cols = []
         for c in range(OWN):
             at = pl.ds(c * k1, k1)
@@ -236,7 +242,7 @@
                 jnp.concatenate([real * twist[0] + imag * twist[1], imag * twist[0] - real * twist[1]], axis=0)
             )
         high, low = split(jnp.concatenate(cols, axis=1))
-        signal = dot(last[0], high) + dot(last[1], high) + dot(last[0], low)
+        signal = dot(last[...], jnp.concatenate([high, high, low], axis=0))
         for c in range(OWN):
             line[pl.ds(c, k1, stride=OWN), :] = signal[:, c * LANES : (c + 1) * LANES]
 
@@ -385,7 +391,7 @@
         vm(parts, F32), vm(parts, F32), vm(parts, BF16), vm(parts, BF16), vm(parts, BF16), vm(parts, BF16),
         vm((nch, rows, chans), BF16),
         vm((k1 * OWN, LANES), F32), vm((k1 * OWN, 2 * LANES), F32), vm((k1 * OWN, 2 * LANES), F32),
-        vm((k1 * OWN, 2 * LANES), BF16), vm((k1 * OWN, 2 * LANES), BF16), vm((rows, mixed), F32),
+        vm((k1 * OWN, 6 * LANES), BF16), vm((rows, mixed), F32),
         vm((2 * feats // LANES, LANES), F32), vm((nch, 2 * feats // LANES, LANES), F32), vm((8, width), F32),
     ]
     dma = pltpu.SemaphoreType.DMA

time: 53.7 us -> 53.6 us (level)
  no operation moved by 1% of the time
where the time goes in v8:
time: 53.6 us; the launch traced here: 53.4 us
  Pallas kernels  52.7 us (98%)
  local copies, waits for them, and re-layouts  0.71 us (1%)
    pallas_call x1, Pallas kernels, shards(): pl.pallas_call(functools.partial(kernel, nctx, nch, 2), out_shape=pltpu.V...  52.7 us

profile of v8, /device:TPU:6, one launch (start us, length us, event | category | flops | bytes accessed | tf_op | source)
XLA Modules:
  0.0 53.4 jit_solution(11275416538219047772)
XLA Ops:
  0.0 52.7 %shard_map.100 = bf16[256,512]{1,0:T(8,128)(2,1)S(1)} custom-call(bf16[256,512]{1,0:T(8,128)(2,1)} %refs_0_.1, bf16[3,4096,256]{2,1,0:T(8,128)(2,1)} %bitcast.2, f32[3,3,256]{2,1,0:T(4,128)} %refs_2_.1, f32[256,256]{1,0:T(8,128)} %refs_3_.1, f32[1,256]{1,0:T(1,128)} %bitcast.3, bf16[2048,512]{1,0:T(8,128)(2,1)} %refs_5_.1, ...), custom_call_target="tpu_custom_call" | custom-call | tf_op jit(solution)/shard_map/pallas_call | solution.py:402
  52.7 0.7 %copy.12 = bf16[256,512]{1,0:T(8,128)(2,1)} copy(bf16[256,512]{1,0:T(8,128)(2,1)S(1)} %shard_map.100) | data formatting | bytes 524288

commit v9 on v8

--- a/solution.py
+++ b/solution.py
@@ -256,12 +256,12 @@
             term = dot(part, w[s, at, :])
             proj[top:, cols] = term if first_one else proj[top:, cols] + term
 
-    x_pull(minus, 0), x_push(minus, 0, plus)
-    x_pull(plus, 1), x_push(plus, 1, minus)
+    x_pull(minus, 0), x_push(minus, 0, plus), x_push(minus, 0, own2, only=0)
+    x_pull(plus, 1), x_push(plus, 1, minus), x_push(plus, 1, own2, only=0)
     hear(2)
     tell(3)
-    x_pull(own2, 0), x_push(own2, 0, plus), x_push(own2, 0, minus, only=0)
-    x_pull(own2, 1), x_push(own2, 1, minus), x_push(own2, 1, plus, only=0)
+    x_pull(own2, 0, only=1), x_push(own2, 0, plus, only=1), x_push(own2, 0, minus, only=1)
+    x_pull(own2, 1, only=1), x_push(own2, 1, minus, only=1), x_push(own2, 1, plus, only=1)
     hear(3)
     tell(4)
     to_next.wait_recv()
@@ -274,18 +274,19 @@
     ]
     for copy in to_ch:
         copy.start()
-    x_pull(minus, 1, only=1), x_push(minus, 1, own2, only=1)
-    x_pull(plus, 0, only=1), x_push(plus, 0, own2, only=1)
+    x_pull(minus, 1, only=0), x_push(minus, 1, own2, only=0)
+    x_pull(plus, 0, only=0), x_push(plus, 0, own2, only=0)
     for h in range(2):
-        x_pull(two, h), x_push(two, h, own2, only=0)
+        x_pull(two, h), x_push(two, h, own2, only=1)
     hear(4)
     for copy in local[2:]:
         copy.wait()
     project(own, True)
+    x_pull(own2, 0, only=0), x_pull(own2, 1, only=0)
     project(own2)
 
-    x_pull(minus2, 0), x_push(minus2, 0, plus, only=1)
-    x_pull(plus2, 1), x_push(plus2, 1, minus, only=1)
+    x_pull(minus2, 0), x_push(minus2, 0, plus, only=0)
+    x_pull(plus2, 1), x_push(plus2, 1, minus, only=0)
     exchange(hsend, hrecv, h_sem)
     others = tails.at[pl.ds(0, nch - 1)]
     pltpu.make_async_copy(others, others, tail_sem.at[1]).wait()
@@ -298,7 +299,7 @@
     for s in range(3):
         before = dot(tail_x[...].astype(BF16), w[s])
         proj[:top, pl.ds(s * chans, chans)] = jnp.where(ctx == 0, 0.0, before)
-    x_pull(minus, 1, only=0), x_pull(plus, 0, only=0)
+    x_pull(minus, 1, only=1), x_pull(plus, 0, only=1)
     for block in (two, minus, plus):
         project(block)
     for block, waits in ((minus2, (1,)), (plus2, (0,)), (two2, (0, 1))):
@@ -396,7 +397,7 @@
     ]
     dma = pltpu.SemaphoreType.DMA
     sems = [
-        pltpu.SemaphoreType.REGULAR((5,)), dma((10,)), dma((18,)), dma((nch, 2)), dma((2,)), dma((2,)), dma((2,)), dma((2,)), dma((2,)),
+        pltpu.SemaphoreType.REGULAR((5,)), dma((10,)), dma((20,)), dma((nch, 2)), dma((2,)), dma((2,)), dma((2,)), dma((2,)), dma((2,)),
         dma((16,)), dma((nch, 2)),
     ]
     return pl.pallas_call(

time: 53.6 us -> 54.5 us (1.017)
  Pallas kernels: 52.7 us -> 53.7 us
    pallas_call x1, Pallas kernels: 52.7 us -> 53.7 us  [shards(): pl.pallas_call(functools.partial(kernel, nctx, nch, 2), out_shape=pltpu.V...]
where the time goes in v9:
time: 54.5 us; the launch traced here: 54.4 us
  Pallas kernels  53.7 us (99%)
  local copies, waits for them, and re-layouts  0.71 us (1%)
    pallas_call x1, Pallas kernels, shards(): pl.pallas_call(functools.partial(kernel, nctx, nch, 2), out_shape=pltpu.V...  53.7 us

profile of v9, /device:TPU:6, one launch (start us, length us, event | category | flops | bytes accessed | tf_op | source)
XLA Modules:
  0.0 54.4 jit_solution(15786962251068185829)
XLA Ops:
  0.0 53.7 %shard_map.100 = bf16[256,512]{1,0:T(8,128)(2,1)S(1)} custom-call(bf16[256,512]{1,0:T(8,128)(2,1)} %refs_0_.1, bf16[3,4096,256]{2,1,0:T(8,128)(2,1)} %bitcast.2, f32[3,3,256]{2,1,0:T(4,128)} %refs_2_.1, f32[256,256]{1,0:T(8,128)} %refs_3_.1, f32[1,256]{1,0:T(1,128)} %bitcast.3, bf16[2048,512]{1,0:T(8,128)(2,1)} %refs_5_.1, ...), custom_call_target="tpu_custom_call" | custom-call | tf_op jit(solution)/shard_map/pallas_call | solution.py:403
  53.7 0.7 %copy.12 = bf16[256,512]{1,0:T(8,128)(2,1)} copy(bf16[256,512]{1,0:T(8,128)(2,1)S(1)} %shard_map.100) | data formatting | bytes 524288
